TPU v7x, 512 devices: a whole 4x4x16 slice. The times are simulated.
512 devices in a mesh: wide: 64 (over y, z_lo, core), narrow: 8 (over z_hi, x).
Axes of the slice: x: 4, y: 4, z: 16 (z_hi: 2, z_lo: 8; z = z_hi * 8 + z_lo), core: 2. Of those that a mesh axis runs over, the one named last changes fastest.
Arguments:
- velocity: float32 [3, 8, 1024, 1024], P(None, 'narrow', 'wide'), may hold values from -6 to 6
- buoyancy: float32 [8, 1024, 1024], P('narrow', 'wide'), may hold values from -6 to 6
- cell_mask: int32 [8, 1024, 1024], P('narrow', 'wide'), may hold values 0 or 1
- spacing: float32 [8], replicated, may hold values from 0.5 to 2
- cotangent: float32 [3, 8, 1024, 1024], P(None, 'narrow', 'wide'), may hold values from -6 to 6
- w_in: float32 [32, 4], replicated, may hold values from -3 to 3
- b_in: float32 [32], replicated, may hold values from -3 to 3
- w_mid: float32 [32, 32], replicated, may hold values from -1 to 1
- b_mid: float32 [32], replicated, may hold values from -3 to 3
- w_out: float32 [3, 32], replicated, may hold values from -1 to 1
Outputs:
- grad_velocity: float32 [3, 8, 1024, 1024], P(None, 'narrow', 'wide')
- grad_buoyancy: float32 [8, 1024, 1024], P('narrow', 'wide')
- grad_w_in: float32 [32, 4], replicated
- grad_b_in: float32 [32], replicated
- grad_w_mid: float32 [32, 32], replicated
- grad_b_mid: float32 [32], replicated
- grad_w_out: float32 [3, 32], replicated
All inputs are finite; a program needn't handle non-finite values. No bound on the sum of `cell_mask` on one device may be relied on, other than what follows from the above.
Results may differ from a plain program's by a relative error of at most 0.0003.
Values sent between devices are 32-bit elements; how exact they have to be, the bound alone decides.
No kernel may reach another device: no remote copies, remote signals or barrier semaphores. Data moves between devices by JAX's collectives and lax.ppermute only.
A program may use at most 64 MiB of HBM per device.

v0:
```python
import functools
import math

import jax
import jax.numpy as jnp
import ml_dtypes
import numpy as np
from jax import lax
from jax.experimental import pallas as pl
from jax.experimental.pallas import tpu as pltpu
from jax.sharding import Mesh
from jax.sharding import PartitionSpec as P

free_surface = 0.05
f32 = jnp.float32
bf16 = jnp.bfloat16
LANES = 128
LEVELS = 8
VMEM_LIMIT = 24 * 1024 * 1024

FINE = (("y", 4), ("zl", 8), ("c", 2), ("zh", 2), ("x", 4))
WIDE = ("y", "zl", "c")
NARROW = ("zh", "x")
PLANE = ("zh", "y", "zl", "c")
SLAB = ("y", "x", "c")
COLUMN = ("zl", "zh")


def dft_table(length):
    indices = np.arange(length)
    frequency = np.minimum(indices, length - indices)
    angle = 2.0 * np.pi / length * (frequency[:, None] * indices[None, :] % length)
    weights = np.where((frequency == 0) | (2 * frequency == length), 1.0, 2.0) / length
    rows_cos = (indices <= length // 2)[:, None]
    return np.where(rows_cos, np.cos(angle), np.sin(angle)) * np.sqrt(weights)[:, None]


def two_parts(table):
    high = table.astype(np.float32).astype(ml_dtypes.bfloat16)
    low = (table - high.astype(np.float64)).astype(np.float32).astype(ml_dtypes.bfloat16)
    return high, low


def eigenvalue(length):
    indices = np.arange(length)
    frequency = np.minimum(indices, length - indices)
    return -4.0 * np.sin(np.pi / length * frequency) ** 2


def split(value):
    high = value.astype(bf16)
    low = (value - high.astype(f32)).astype(bf16)
    return high, low


def split_f32(value):
    high = value.astype(bf16).astype(f32)
    return high, value - high


def dot(a, b):
    return jnp.dot(a, b, preferred_element_type=f32)


def dot_nt(a, b):
    return lax.dot_general(a, b, (((1,), (1,)), ((), ())), preferred_element_type=f32)


def roll(value, shift, axis):
    size = value.shape[axis]
    shift = shift % size
    return value if shift == 0 else pltpu.roll(value, shift, axis)


def lane_of(shape):
    return lax.broadcasted_iota(jnp.int32, shape, len(shape) - 1)


def start_copy(source, target, sems, index):
    copy = pltpu.make_async_copy(source, target, sems.at[index])
    copy.start()
    return copy


def call(kernel, out_shape, args, smem=(), hbm=(), hbm_out=(), scratch=(), flops=0, name=None):
    def space(index, held):
        return pl.BlockSpec(memory_space=held.get(index, pltpu.VMEM))

    held = {i: pltpu.SMEM for i in smem} | {i: pl.ANY for i in hbm}
    args = [
        pltpu.with_memory_space_constraint(a, pltpu.HBM) if i in hbm else a
        for i, a in enumerate(args)
    ]
    moved = sum(int(np.prod(a.shape)) * a.dtype.itemsize for a in args)
    return pl.pallas_call(
        kernel,
        out_shape=out_shape,
        in_specs=[space(i, held) for i in range(len(args))],
        out_specs=[space(i, {o: pl.ANY for o in hbm_out}) for i in range(len(out_shape))],
        scratch_shapes=list(scratch),
        compiler_params=pltpu.CompilerParams(vmem_limit_bytes=VMEM_LIMIT),
        cost_estimate=pl.CostEstimate(flops=flops, bytes_accessed=moved, transcendentals=0),
        name=name,
    )(*args)


def forward_x(cot_hbm, high_hbm, low_hbm, out_ref, mark_ref, high_ref, low_ref, cot_ref, sems):
    first = start_copy(cot_hbm, cot_ref, sems, 16)
    blocks = [slice(LANES * t, LANES * (t + 1)) for t in range(8)]
    copies = []
    for t, block in enumerate(blocks):
        copies.append(
            (
                start_copy(high_hbm.at[block, :], high_ref.at[block, :], sems, 2 * t),
                start_copy(low_hbm.at[block, :], low_ref.at[block, :], sems, 2 * t + 1),
            )
        )
    first.wait()
    east, north, up = cot_ref[0, 0], cot_ref[1, 0], cot_ref[2, 0]
    rows, width = east.shape
    east = east - roll(east, -1, 1)
    high, low = split_f32(jnp.concatenate([east, north, up], axis=0))
    none = jnp.zeros((rows, width), f32)
    both = jnp.concatenate([high, none, low, none], axis=0).T.astype(bf16)
    lane = lane_of((LANES, LANES))
    packed = [jnp.zeros((LANES, LANES), f32)] * 3
    for t, block in enumerate(blocks):
        for copy in copies[t]:
            copy.wait()
        got = dot(high_ref[block, :], both) + dot(low_ref[block, :], both)
        got = got + roll(got, 64, 1)
        for field in range(3):
            packed[field] = jnp.where(
                lane // 16 == t, roll(got, 16 * (t - field), 1), packed[field]
            )
    for field in range(3):
        out_ref[:, 0, LANES * field : LANES * (field + 1)] = packed[field]
    mark_ref[...] = jnp.zeros(mark_ref.shape, f32)


def forward_y(msg_ref, high_hbm, low_hbm, mark_ref, out_ref, line_ref, high_ref, low_ref, sems):
    blocks = [slice(256 * g, 256 * (g + 1)) for g in range(4)]
    copies = [
        (
            start_copy(high_hbm.at[block, :], high_ref.at[block, :], sems, 2 * g),
            start_copy(low_hbm.at[block, :], low_ref.at[block, :], sems, 2 * g + 1),
        )
        for g, block in enumerate(blocks)
    ]
    lane = lane_of((64, LANES))
    within = lane % 16
    highs = []
    lows = []
    for half in range(2):
        part = slice(64 * half, 64 * (half + 1))
        east = msg_ref[part, 0, 0:LANES]
        north = msg_ref[part, 0, LANES : 2 * LANES]
        up = msg_ref[part, 0, 2 * LANES : 3 * LANES]
        after = jnp.where(
            within < 15, roll(north, -1, 1), roll(roll(north, -1, 0), 15, 1)
        )
        for value in (east + north - after, up):
            high, low = split_f32(value)
            highs.append(high)
            lows.append(low)
    shifted = [roll(value, c, 1) for c, value in enumerate(highs + lows)]
    for j in range(16):
        line = jnp.zeros((64, LANES), f32)
        for c, value in enumerate(shifted):
            line = jnp.where(within == (c + j) % 16, value, line)
        line_ref[pl.ds(j, 64, stride=16), :] = roll(line, -j, 1)
    lines = line_ref[...].astype(bf16)
    lane = lane_of((256, LANES))
    packed = jnp.zeros((256, LANES), f32)
    for g, block in enumerate(blocks):
        for copy in copies[g]:
            copy.wait()
        got = dot(high_ref[block, :], lines) + dot(low_ref[block, :], lines)
        got = got + roll(got, -4, 1)
        packed = jnp.where(lane % 16 // 4 == g, roll(got, 4 * g, 1), packed)
    for peer in range(4):
        out_ref[peer] = packed


def vertical(spacing):
    one = jnp.ones((1, LANES), f32)
    none = jnp.zeros((1, LANES), f32)
    spacing = [one * spacing[k] for k in range(LEVELS)]
    inv_dz = [1.0 / value for value in spacing]
    face = [2.0 / (spacing[k] + spacing[k + 1]) for k in range(LEVELS - 1)] + [none]
    lower = [none] + [inv_dz[k] * face[k - 1] for k in range(1, LEVELS)]
    upper = [inv_dz[k] * face[k] for k in range(LEVELS)]
    base = [-(lower[k] + upper[k]) for k in range(LEVELS)]
    base[-1] = base[-1] - free_surface * inv_dz[-1]
    sub = [none] + upper[:-1]
    sup = lower[1:] + [none]
    keep = [one] * (LEVELS - 1) + [none]
    return inv_dz, face, sub, base, sup, keep


def solve_back(spacing_ref, got_ref, lam_hbm, high_hbm, low_hbm, out_ref,
               lam_ref, high_ref, low_ref, sems):
    lam_copy = start_copy(lam_hbm, lam_ref, sems, 16)
    copies = []
    for pair in range(8):
        block = slice(LANES * pair, LANES * (pair + 1))
        copies.append(
            (
                start_copy(high_hbm.at[block, :], high_ref.at[block, :], sems, 2 * pair),
                start_copy(low_hbm.at[block, :], low_ref.at[block, :], sems, 2 * pair + 1),
            )
        )
    lam_copy.wait()
    at = lax.axis_index("x")
    lam = lam_ref[...]
    rows = lam.shape[0]
    lane = lane_of((rows, LANES))
    inv_dz, face, sub, base, sup, keep = vertical([spacing_ref[k] for k in range(LEVELS)])
    ratios = []
    values = []
    below = None
    for k in range(LEVELS):
        packed = got_ref[k % 4]
        half = k // 4
        flux = roll(packed, -(2 * half + 1), 1) * face[k]
        right = roll(packed, -2 * half, 1) - flux
        if k > 0:
            right = right + below
        below = flux
        diagonal = lam + base[k]
        if k > 0:
            diagonal = diagonal - sub[k] * ratios[-1]
            right = right - sub[k] * values[-1]
        inverse = 1.0 / diagonal
        ratios.append(sup[k] * inverse)
        values.append(right * inverse)
    result = [None] * LEVELS
    result[-1] = values[-1]
    for k in range(LEVELS - 2, -1, -1):
        result[k] = values[k] - ratios[k] * result[k + 1]
    scaled = [result[k] * inv_dz[k] for k in range(LEVELS)] + [jnp.zeros_like(lam)]
    change = [(scaled[k] - scaled[k + 1]) * keep[k] for k in range(LEVELS)]

    def own(items, half):
        value = items[4 * half]
        for x in range(1, 4):
            value = jnp.where(at == x, items[4 * half + x], value)
        return value

    column = lane % 4
    both = own(result, 0)
    both = jnp.where(column == 1, roll(own(change, 0), 1, 1), both)
    both = jnp.where(column == 2, roll(own(result, 1), 2, 1), both)
    both = jnp.where(column == 3, roll(own(change, 1), 3, 1), both)
    high, low = split_f32(both)
    blocks = [
        jnp.where(lane % 16 < 4, roll(high, -4 * g, 1), roll(low, 4 - 4 * g, 1)).astype(bf16)
        for g in range(4)
    ]
    columns = jnp.concatenate(blocks, axis=0)
    within = lane_of((64, LANES)) % 16
    packed = [jnp.zeros((64, LANES), f32)] * 4
    for pair in range(8):
        block = slice(LANES * pair, LANES * (pair + 1))
        for copy in copies[pair]:
            copy.wait()
        got = dot(high_ref[block, :], columns) + dot(low_ref[block, :], columns)
        got = got + roll(got, -4, 1)
        for one in range(2):
            j = 2 * pair + one
            moved = roll(got[64 * one : 64 * (one + 1)], j, 1)
            for c in range(4):
                packed[c] = jnp.where(within == (j + c) % 16, moved, packed[c])
    for half in range(2):
        part = slice(64 * half, 64 * (half + 1))
        pressure = roll(packed[2 * half], -2 * half, 1)
        change_up = roll(packed[2 * half + 1], -(2 * half + 1), 1)
        before = jnp.where(
            within > 0, roll(pressure, 1, 1), roll(roll(pressure, 1, 0), -15, 1)
        )
        out_ref[part, 0, 0:LANES] = pressure
        out_ref[part, 0, LANES : 2 * LANES] = change_up
        out_ref[part, 0, 2 * LANES : 3 * LANES] = before - pressure


CHUNK = 256


def unit_rows(shape, axis):
    return lax.broadcasted_iota(jnp.int32, shape, axis) % 8


def same_row(value):
    shape = value.shape
    return jnp.where(unit_rows(shape, 0) == unit_rows(shape, 1), value, 0.0)


def gather(shape, step):
    to = lax.broadcasted_iota(jnp.int32, shape, 1)
    return (lax.broadcasted_iota(jnp.int32, shape, 0) // step == to).astype(f32)


def exact(a, b):
    return jnp.dot(a, b, precision=lax.Precision.HIGHEST, preferred_element_type=f32)


def spread(weight, columns):
    tall, wide = weight.shape
    step = (
        lax.broadcasted_iota(jnp.int32, (wide, columns), 1) // 8
        == lax.broadcasted_iota(jnp.int32, (wide, columns), 0)
    ).astype(f32)
    value = exact(weight, step)
    value = jnp.broadcast_to(value[:, None, :], (tall, 8, columns)).reshape(8 * tall, columns)
    return same_row(value)


def closure_forward(vel_hbm, buoy_hbm, win_ref, bin_ref, wmid_ref, bmid_ref, wout_ref,
                    ey_hbm, ex_hbm, mark_ref,
                    f1h_hbm, f1l_hbm, f2h_hbm, f2l_hbm, ft_hbm, wide_hbm, win_hbm, lam_hbm, done_ref,
                    f1h_ref, f1l_ref, f2h_ref, f2l_ref, ft_ref, wide_ref, in_ref, lam_ref,
                    vel_ref, buoy_ref, ex_ref, sems, out_sems):
    copies = [
        start_copy(vel_hbm, vel_ref, sems, 0),
        start_copy(buoy_hbm, buoy_ref, sems, 1),
        start_copy(ex_hbm, ex_ref, sems, 2),
        start_copy(ey_hbm, lam_ref, sems, 3),
    ]
    win_t = win_ref[...]
    wmid = wmid_ref[...]
    wout_h, wout_l = split_f32(spread(wout_ref[...].T, 32))
    wide_ref[:, 0:96] = jnp.concatenate([wout_h, wout_h, wout_l], axis=1).astype(bf16)
    wide_ref[:, 96:128] = jnp.zeros((256, 32), bf16)
    wide_ref[:, 128:384], wide_ref[:, 384:640] = split(spread(wmid.T, 256))
    in_ref[:, 0:256], in_ref[:, 256:512] = split(spread(win_t, 256))
    win_h, win_l = split_f32(spread(win_t.T, 32))
    win_cat = jnp.concatenate([win_h, win_h, win_l], axis=1).astype(bf16)
    wmh, wml = split(spread(wmid, 256))

    def tall(row):
        column = row.T
        return jnp.broadcast_to(column[:, None, :], (32, 8, 1)).reshape(256, 1)

    b_in, b_mid = tall(bin_ref[...]), tall(bmid_ref[...])
    for copy in copies:
        copy.wait()
    lam_ref[...] = lam_ref[...] + ex_ref[pl.ds(lax.axis_index(PLANE), 1), :]
    copies = [
        start_copy(wide_ref, wide_hbm, out_sems, 0),
        start_copy(in_ref, win_hbm, out_sems, 1),
        start_copy(lam_ref, lam_hbm, out_sems, 2),
    ]
    width = buoy_ref.shape[-1]
    for half in range(2):
        part = slice(8 * half, 8 * (half + 1))
        for start in range(0, width, CHUNK):
            col = slice(start, start + CHUNK)
            to = slice(half * width + start, half * width + start + CHUNK)
            feats = jnp.concatenate(
                [vel_ref[c, 0, part, col] for c in range(3)] + [buoy_ref[0, part, col]], axis=0
            )
            high, low = split_f32(feats)
            stack = jnp.concatenate([high, low, high], axis=0).astype(bf16)
            ft_ref[:, to] = jnp.concatenate(
                [high, low, jnp.ones((32, CHUNK), f32)], axis=0
            ).astype(bf16)
            first = jnp.tanh(dot(win_cat, stack) + b_in)
            fh, fl = split(first)
            f1h_ref[:, to] = fh
            f1l_ref[:, to] = fl
            second = dot(wmh, fh) + dot(wmh, fl) + dot(wml, fh)
            second = jnp.tanh(second + b_mid)
            sh, sl = split(second)
            f2h_ref[:, to] = sh
            f2l_ref[:, to] = sl
        whole = slice(half * width, (half + 1) * width)
        for i, (held, target) in enumerate(
            (
                (f1h_ref, f1h_hbm),
                (f1l_ref, f1l_hbm),
                (f2h_ref, f2h_hbm),
                (f2l_ref, f2l_hbm),
                (ft_ref, ft_hbm),
            )
        ):
            copies.append(
                start_copy(held.at[:, whole], target.at[:, whole], out_sems, 3 + 5 * half + i)
            )
    done_ref[...] = jnp.zeros(done_ref.shape, f32)
    for copy in copies:
        copy.wait()


def closure_back(msg_ref, high_hbm, low_hbm, cot_hbm, mask_hbm,
                 f1h_hbm, f1l_hbm, f2h_hbm, f2l_hbm, ft_hbm, wide_hbm,
                 total_ref, e1h_hbm, e1l_hbm, proj_hbm,
                 high_ref, low_ref, cot_ref, mask_ref,
                 f1h_ref, f1l_ref, f2h_ref, f2l_ref, ft_ref, wide_ref,
                 e1h_ref, e1l_ref, proj_ref, e2h_ref, e2l_ref, dl_ref, b2_ref, sems, out_sems):
    width = mask_ref.shape[-1]
    table_copies = [start_copy(high_hbm, high_ref, sems, 0), start_copy(low_hbm, low_ref, sems, 1)]
    copies = [
        start_copy(cot_hbm, cot_ref, sems, 2),
        start_copy(mask_hbm, mask_ref, sems, 3),
        start_copy(wide_hbm, wide_ref, sems, 4),
    ]
    hidden_copies = []
    for half in range(2):
        whole = slice(half * width, (half + 1) * width)
        hidden_copies.append(
            [
                start_copy(held.at[:, whole], target.at[:, whole], sems, 5 + 4 * half + i)
                for i, (held, target) in enumerate(
                    (
                        (f2h_hbm, f2h_ref),
                        (f2l_hbm, f2l_ref),
                        (f1h_hbm, f1h_ref),
                        (f1l_hbm, f1l_ref),
                    )
                )
            ]
        )
    ft_copy = start_copy(ft_hbm, ft_ref, sems, 13)
    lane = lane_of((LANES, LANES))
    columns = []
    for t in range(8):
        value = jnp.zeros((LANES, LANES), f32)
        for field in range(3):
            item = msg_ref[:, 0, LANES * field : LANES * (field + 1)]
            value = jnp.where(lane // 16 == field, roll(item, 16 * (field - t), 1), value)
        high, low = split_f32(value)
        columns.append((high + roll(low, 64, 1)).T.astype(bf16))
    columns = jnp.concatenate(columns, axis=1)
    for copy in table_copies:
        copy.wait()
    field = dot(columns, high_ref[...]) + dot(columns, low_ref[...])
    pressure = field[0:16] + field[64:80]
    east_back = roll(pressure, 1, 1) - pressure
    for copy in copies:
        copy.wait()
    projected = (
        cot_ref[0, 0] - east_back,
        cot_ref[1, 0] - (field[32:48] + field[96:112]),
        cot_ref[2, 0] - (field[16:32] + field[80:96]),
    )
    wet = mask_ref[0].astype(f32)
    for c in range(3):
        proj_ref[c, 0] = projected[c]
    out_copies = [start_copy(proj_ref, proj_hbm, out_sems, 0)]
    deltas = [value * wet for value in projected]
    blank = jnp.zeros((8, CHUNK), f32)
    bias2 = jnp.zeros((256, LANES), f32)
    for half in range(2):
        part = slice(8 * half, 8 * (half + 1))
        for copy in hidden_copies[half]:
            copy.wait()
        for start in range(0, width, CHUNK):
            col = slice(start, start + CHUNK)
            to = slice(half * width + start, half * width + start + CHUNK)
            delta = jnp.concatenate([value[part, col] for value in deltas] + [blank], axis=0)
            dh, dl = split_f32(delta)
            stack = jnp.concatenate([dh, dl, dh], axis=0).astype(bf16)
            dl_ref[:, to] = stack[0:64]
            second = f2h_ref[:, to].astype(f32) + f2l_ref[:, to].astype(f32)
            err2 = dot(wide_ref[:, 0:96], stack) * (1.0 - second * second)
            bias2 = bias2 + err2[:, 0:LANES] + err2[:, LANES : 2 * LANES]
            e2h, e2l = split(err2)
            e2h_ref[:, to] = e2h
            e2l_ref[:, to] = e2l
            first = f1h_ref[:, to].astype(f32) + f1l_ref[:, to].astype(f32)
            err1 = (
                dot(wide_ref[:, 128:384], e2h)
                + dot(wide_ref[:, 128:384], e2l)
                + dot(wide_ref[:, 384:640], e2h)
            )
            err1 = err1 * (1.0 - first * first)
            e1h, e1l = split(err1)
            e1h_ref[:, to] = e1h
            e1l_ref[:, to] = e1l
        whole = slice(half * width, (half + 1) * width)
        out_copies.append(
            start_copy(e1h_ref.at[:, whole], e1h_hbm.at[:, whole], out_sems, 1 + 2 * half)
        )
        out_copies.append(
            start_copy(e1l_ref.at[:, whole], e1l_hbm.at[:, whole], out_sems, 2 + 2 * half)
        )
    b2_ref[...] = bias2
    ft_copy.wait()
    mid = (
        dot_nt(e2h_ref[...], f1h_ref[...])
        + dot_nt(e2h_ref[...], f1l_ref[...])
        + dot_nt(e2l_ref[...], f1h_ref[...])
    )
    both1 = dot_nt(e1h_ref[...], ft_ref[...])
    rest1 = dot_nt(e1l_ref[...], ft_ref[...])
    win = both1[:, 0:32] + both1[:, 32:64] + rest1[:, 0:32]
    bin_ = both1[:, 64:96] + rest1[:, 64:96]
    both2 = dot_nt(f2h_ref[...], dl_ref[...])
    rest2 = dot_nt(f2l_ref[...], dl_ref[...])
    wout = both2[:, 0:32] + both2[:, 32:64] + rest2[:, 0:32]

    def fold_rows(value):
        return jnp.sum(value.reshape(32, 8, value.shape[1]), axis=1)

    mid = exact(fold_rows(same_row(mid)), gather((256, LANES), 8))
    small = jnp.concatenate(
        [
            fold_rows(same_row(win)),
            fold_rows(same_row(wout)),
            fold_rows(jnp.where(lane_of((256, 32)) == 0, bin_, 0.0)),
        ],
        axis=1,
    )
    small = roll(exact(small, gather((96, LANES), 8)), 32, 1)
    b2 = jnp.sum(fold_rows(b2_ref[...]), axis=1, keepdims=True)
    every = mid + small + jnp.where(lane_of((32, LANES)) == 39, b2, 0.0)
    units = jnp.concatenate([every[8 * i : 8 * (i + 1), 0:32] for i in range(4)], axis=1)
    turned = every.T
    rows = [units[i : i + 1] for i in range(8)]
    for start in (32, 36):
        rows.append(
            jnp.concatenate([turned[start + i : start + i + 1] for i in range(4)], axis=1)
        )
    rows.append(jnp.concatenate([turned[40:41], jnp.zeros((1, 96), f32)], axis=1))
    for peer in range(32):
        for i, row in enumerate(rows):
            total_ref[peer, :, LANES * i : LANES * (i + 1)] = row
    for copy in out_copies:
        copy.wait()


def outgoing(proj_hbm, e1h_hbm, e1l_hbm, win_hbm, mark_ref, gvel_ref, gbuoy_ref,
             proj_ref, e1h_ref, e1l_ref, win_ref, sems):
    copies = [
        start_copy(proj_hbm, proj_ref, sems, 0),
        start_copy(e1h_hbm, e1h_ref, sems, 1),
        start_copy(e1l_hbm, e1l_ref, sems, 2),
        start_copy(win_hbm, win_ref, sems, 3),
    ]
    for copy in copies:
        copy.wait()
    width = gbuoy_ref.shape[-1]
    for half in range(2):
        part = slice(8 * half, 8 * (half + 1))
        to = slice(half * width, (half + 1) * width)
        out = (
            dot(win_ref[:, 0:256], e1h_ref[:, to])
            + dot(win_ref[:, 0:256], e1l_ref[:, to])
            + dot(win_ref[:, 256:512], e1h_ref[:, to])
        )
        for c in range(3):
            gvel_ref[c, 0, part, :] = proj_ref[c, 0, part, :] + out[8 * c : 8 * (c + 1)]
        gbuoy_ref[0, part, :] = out[24:32]


def sum_slab(got_ref, out_ref, mark_ref):
    total = jnp.sum(got_ref[...], axis=0)
    for peer in range(16):
        out_ref[peer] = total
    mark_ref[...] = jnp.zeros(mark_ref.shape, f32)


def sum_column(scale, got_ref, win_ref, bin_ref, wmid_ref, bmid_ref, wout_ref):
    total = jnp.sum(got_ref[...], axis=0) * scale
    rows = [total[:, LANES * i : LANES * (i + 1)] for i in range(11)]
    units = jnp.concatenate(rows[:8], axis=0)
    wmid_ref[...] = jnp.concatenate([units[:, 32 * i : 32 * (i + 1)] for i in range(4)], axis=0)
    win_ref[...] = jnp.concatenate([rows[8][:, 32 * i : 32 * (i + 1)] for i in range(4)], axis=0)
    wout_ref[...] = jnp.concatenate([rows[9][:, 32 * i : 32 * (i + 1)] for i in range(3)], axis=0)
    bmid_ref[...] = rows[9][:, 96:128]
    bin_ref[...] = rows[10][:, 0:32]


def shards(velocity, buoyancy, cell_mask, spacing, cotangent, w_in, b_in, w_mid, b_mid, w_out):
    levels, rows, width = buoyancy.shape
    depth = spacing.shape[0]
    span_y = rows * 64
    order = (np.arange(1024) % 128) * 8 + np.arange(1024) // 128
    table = dft_table(width)[order]
    x_high, x_low = two_parts(table)
    row_order = (np.arange(1024) % 64) * 16 + np.arange(1024) // 64
    y_high, y_low = two_parts(table[:, row_order].T)
    eigen = eigenvalue(width)
    lanes = np.arange(LANES)
    ey = eigen[order].reshape(4, 256)[lanes % 16 // 4].T.astype(np.float32)
    ex = eigen[(8 * np.arange(128))[:, None] + lanes[None, :] // 16].astype(np.float32)
    x_high, x_low, y_high, y_low, ey, ex = map(
        jnp.asarray, (x_high, x_low, y_high, y_low, ey, ex)
    )
    cells = rows * width // 8
    dma = pltpu.SemaphoreType.DMA
    type_of = jax.ShapeDtypeStruct
    table = pltpu.VMEM((1024, 1024), bf16)
    wide = pltpu.VMEM((256, cells), bf16)
    wide_type = pltpu.HBM((256, cells), bf16)
    mark_type = type_of((8, LANES), f32)
    table_flops = 4 * 1024 * 1024 * 128
    msg_type = type_of((128, 1, 3 * LANES), f32)
    msg, mark = call(
        forward_x,
        (msg_type, mark_type),
        (cotangent, x_high, x_low),
        hbm=(0, 1, 2),
        scratch=(table, table, pltpu.VMEM(cotangent.shape, f32), dma((17,))),
        flops=table_flops,
        name="forward_x",
    )
    msg = lax.all_to_all(msg, PLANE, 0, 0)

    *hidden, wide_w, win_w, lam, mark = call(
        closure_forward,
        (
            (wide_type,) * 4
            + (
                pltpu.HBM((96, cells), bf16),
                pltpu.HBM((256, 640), bf16),
                pltpu.HBM((32, 512), bf16),
                pltpu.HBM((256, LANES), f32),
                mark_type,
            )
        ),
        (velocity, buoyancy, w_in.T, b_in[None], w_mid, b_mid[None], w_out, ey, ex, mark),
        hbm=(0, 1, 7, 8),
        hbm_out=range(8),
        scratch=(wide,) * 4
        + (
            pltpu.VMEM((96, cells), bf16),
            pltpu.VMEM((256, 640), bf16),
            pltpu.VMEM((32, 512), bf16),
            pltpu.VMEM((256, LANES), f32),
            pltpu.VMEM(velocity.shape, f32),
            pltpu.VMEM(buoyancy.shape, f32),
            pltpu.VMEM((LANES, LANES), f32),
            dma((4,)),
            dma((13,)),
        ),
        flops=2 * 256 * 256 * cells * 4,
        name="closure_forward",
    )
    (gathered,) = call(
        forward_y,
        (type_of((4, 256, LANES), f32),),
        (msg, x_high, x_low, mark),
        hbm=(1, 2),
        scratch=(pltpu.VMEM((1024, LANES), f32), table, table, dma((8,))),
        flops=table_flops,
        name="forward_y",
    )
    gathered = lax.all_to_all(gathered, "x", 0, 0)
    (msg,) = call(
        solve_back,
        (msg_type,),
        (spacing, gathered, lam, y_high, y_low),
        smem=(0,),
        hbm=(2, 3, 4),
        scratch=(pltpu.VMEM((256, LANES), f32), table, table, dma((17,))),
        flops=table_flops,
        name="solve_back",
    )
    msg = lax.all_to_all(msg, PLANE, 0, 0)
    totals, e1h, e1l, projected = call(
        closure_back,
        (
            type_of((32, 1, 11 * LANES), f32),
            wide_type,
            wide_type,
            pltpu.HBM(cotangent.shape, f32),
        ),
        (msg, x_high, x_low, cotangent, cell_mask, *hidden, wide_w),
        hbm=range(1, 11),
        hbm_out=(1, 2, 3),
        scratch=(
            table,
            table,
            pltpu.VMEM(cotangent.shape, f32),
            pltpu.VMEM(cell_mask.shape, jnp.int32),
            wide,
            wide,
            wide,
            wide,
            pltpu.VMEM((96, cells), bf16),
            pltpu.VMEM((256, 640), bf16),
            wide,
            wide,
            pltpu.VMEM(cotangent.shape, f32),
            wide,
            wide,
            pltpu.VMEM((64, cells), bf16),
            pltpu.VMEM((256, LANES), f32),
            dma((14,)),
            dma((5,)),
        ),
        flops=table_flops + 2 * 256 * 256 * cells * 10,
        name="closure_back",
    )
    totals = lax.all_to_all(totals, SLAB, 0, 0)
    totals, mark = call(
        sum_slab, (type_of((16, 1, 11 * LANES), f32), mark_type), (totals,), name="sum_slab"
    )
    totals = lax.all_to_all(totals, COLUMN, 0, 0)
    grad_velocity, grad_buoyancy = call(
        outgoing,
        (type_of(cotangent.shape, f32), type_of(buoyancy.shape, f32)),
        (projected, e1h, e1l, win_w, mark),
        hbm=(0, 1, 2, 3),
        scratch=(
            pltpu.VMEM(cotangent.shape, f32),
            wide,
            wide,
            pltpu.VMEM((32, 512), bf16),
            dma((4,)),
        ),
        flops=2 * 256 * 256 * cells,
        name="outgoing",
    )
    scale = 1.0 / math.sqrt(width * span_y * depth)
    grad_in, grad_b_in, grad_mid, grad_b_mid, grad_out = call(
        functools.partial(sum_column, scale),
        (
            type_of((4, 32), f32),
            type_of((1, 32), f32),
            type_of((32, 32), f32),
            type_of((1, 32), f32),
            type_of((3, 32), f32),
        ),
        (totals,),
        name="sum_column",
    )
    return (
        grad_velocity,
        grad_buoyancy,
        grad_in.T,
        grad_b_in[0],
        grad_mid,
        grad_b_mid[0],
        grad_out,
    )


def solution(mesh):
    fine = Mesh(
        mesh.devices.reshape([size for _, size in FINE]), tuple(name for name, _ in FINE)
    )
    field = P(None, NARROW, WIDE, None)
    cell = P(NARROW, WIDE, None)
    in_specs = (field, cell, cell, P(), field, P(), P(), P(), P(), P())
    out_specs = (field, cell, P(), P(), P(), P(), P())
    return jax.shard_map(shards, mesh=fine, in_specs=in_specs, out_specs=out_specs, check_vma=False)
```

profile of v0, /device:TPU:32, one launch (start us, length us, event | category | flops | bytes accessed | tf_op | source)
XLA Modules:
  0.0 136.2 jit_solution(10961243442922530718)
XLA Ops:
  0.6 0.0 copy-start.3
  0.6 0.0 copy-start.5
  0.7 0.0 copy-start.1
  0.7 0.0 copy-start.4
  0.7 0.0 copy-start.2
  0.7 5.6 %forward_x.1 = (f32[128,1,384]{2,1,0:T(1,128)}, f32[8,128]{1,0:T(8,128)S(1)}) custom-call(f32[3,1,16,1024]{3,2,1,0:T(8,128)} %cot_hbm.3, bf16[1024,1024]{1,0:T(8,128)(2,1)} %constant.12.clone.high_hbm, bf16[1024,1024]{1,0:T(8,128)(2,1)} %constant.13.clone.low_hbm), custom_call_target="tpu_custom_call" | custom-call | flops 536870912 | bytes 4390912 | tf_op jit(solution)/shard_map/forward_x/pallas_call | solution.py:95
  6.3 19.2 %all-to-all-start = ((f32[128,1,384]{2,1,0:T(1,128)}), f32[128,1,384]{2,1,0:T(1,128)S(1)}, u32[]{:S(2)}, u32[]{:S(2)}) async-start(f32[128,1,384]{2,1,0:T(1,128)} %get-tuple-element.31), calls=%async_computation | async-start | bytes 393216 | tf_op jit(solution)/shard_map/all_to_all | solution.py:608
  25.5 0.0 copy-done.3
  25.5 0.0 copy-done.5
  25.5 0.0 copy-done.1
  25.5 0.0 copy-done.4
  25.5 0.0 copy-done.2
  25.5 5.0 %closure_forward.1 = (bf16[256,2048]{1,0:T(8,128)(2,1)}, bf16[256,2048]{1,0:T(8,128)(2,1)}, bf16[256,2048]{1,0:T(8,128)(2,1)}, bf16[256,2048]{1,0:T(8,128)(2,1)}...) custom-call(f32[3,1,16,1024]{3,2,1,0:T(8,128)} %vel_hbm.1, ...), custom_call_target="tpu_custom_call" | custom-call | flops 1073741824 | bytes 468096 | tf_op jit(solution)/shard_map/closure_forward/pallas_call | solution.py:95
  30.6 15.6 %all-to-all-done.msg_ref = f32[128,1,384]{2,1,0:T(1,128)S(1)} async-done(((f32[128,1,384]{2,1,0:T(1,128)}), f32[128,1,384]{2,1,0:T(1,128)S(1)}, u32[]{:S(2)}, u32[]{:S(2)}) %all-to-all-start) | async-done | bytes 196640 | tf_op jit(solution)/shard_map/all_to_all | solution.py:608
  46.1 0.0 copy-start
  46.1 3.5 %forward_y.1 = f32[4,256,128]{2,1,0:T(8,128)S(1)} custom-call(f32[128,1,384]{2,1,0:T(1,128)S(1)} %all-to-all-done.msg_ref, bf16[1024,1024]{1,0:T(8,128)(2,1)} %constant.12.clone.high_hbm, bf16[1024,1024]{1,0:T(8,128)(2,1)} %constant.13.clone.low_hbm, f32[8,128]{1,0:T(8,128)S(1)} %get-tuple-element.33.mark_ref), custom_call_target="tpu_custom_call" | custom-call | flops 536870912 | bytes 4395008 | tf_op jit(solution)/shard_map/forward_y/pallas_call | solution.py:95
  49.6 12.8 %all_to_all.25.got_ref = f32[4,256,128]{2,1,0:T(8,128)S(1)} all-to-all(f32[4,256,128]{2,1,0:T(8,128)S(1)} %forward_y.1), channel_id=1, replica_groups=mesh['y'=4,'zl'=8,'c'=2,'zh'=2,'x'=4] {'x'}, dimensions={0} | all-to-all | bytes 1048576 | tf_op jit(solution)/shard_map/all_to_all | solution.py:649
  62.4 0.0 copy-done
  62.4 6.2 %solve_back.1 = f32[128,1,384]{2,1,0:T(1,128)S(1)} custom-call(f32[8]{0:T(128)S(1)} %copy-done, f32[4,256,128]{2,1,0:T(8,128)S(1)} %all_to_all.25.got_ref, f32[256,128]{1,0:T(8,128)} %get-tuple-element.34.lam_hbm, bf16[1024,1024]{1,0:T(8,128)(2,1)} %constant.14.clone.high_hbm, bf16[1024,1024]{1,0:T(8,128)(2,1)} %constant.15.clone.low_hbm), custom_call_target="tpu_custom_call" | custom-call | flops 536870912 | bytes 4849696 | tf_op jit(solution)/shard_map/solve_back/pallas_call | solution.py:95
  68.6 26.9 %all_to_all.26.msg_ref = f32[128,1,384]{2,1,0:T(1,128)S(1)} all-to-all(f32[128,1,384]{2,1,0:T(1,128)S(1)} %solve_back.1), channel_id=1, replica_groups=mesh['y'=4,'zl'=8,'c'=2,'zh'=2,'x'=4] {'zh','y','zl','c'}, dimensions={0} | all-to-all | bytes 393216 | tf_op jit(solution)/shard_map/all_to_all | solution.py:660
  95.5 9.3 %closure_back.1 = (f32[32,1,1408]{2,1,0:T(1,128)S(1)}, bf16[256,2048]{1,0:T(8,128)(2,1)}, bf16[256,2048]{1,0:T(8,128)(2,1)}, f32[3,1,16,1024]{3,2,1,0:T(8,128)}) custom-call(f32[128,1,384]{2,1,0:T(1,128)S(1)} %all_to_all.26.msg_ref, bf16[1024,1024]{1,0:T(8,128)(2,1)} %constant.12.clone.high_hbm, bf16[1024,1024]{1,0:T(8,128)(2,1)} %constant.13.clone.low_hbm, ...), custom_call_target="tpu_custom_call" | custom-call | flops 3221225472 | bytes 9568256 | tf_op jit(solution)/shard_map/closure_back/pallas_call | solution.py:95
  104.8 11.1 %all_to_all.27.got_ref = f32[32,1,1408]{2,1,0:T(1,128)S(1)} all-to-all(f32[32,1,1408]{2,1,0:T(1,128)S(1)} %get-tuple-element.45), channel_id=1, replica_groups=mesh['y'=4,'zl'=8,'c'=2,'zh'=2,'x'=4] {'y','x','c'}, dimensions={0} | all-to-all | bytes 360448 | tf_op jit(solution)/shard_map/all_to_all | solution.py:696
  115.8 0.8 sum_slab.1
  116.6 4.6 %all-to-all-start.4 = ((f32[16,1,1408]{2,1,0:T(1,128)}), f32[16,1,1408]{2,1,0:T(1,128)S(1)}, u32[]{:S(2)}, u32[]{:S(2)}) async-start(f32[16,1,1408]{2,1,0:T(1,128)} %get-tuple-element.49), calls=%async_computation.4 | async-start | bytes 180224 | tf_op jit(solution)/shard_map/all_to_all | solution.py:700
  121.2 3.0 %outgoing.1 = (f32[3,1,16,1024]{3,2,1,0:T(8,128)}, f32[1,16,1024]{2,1,0:T(8,128)}) custom-call(f32[3,1,16,1024]{3,2,1,0:T(8,128)} %get-tuple-element.41.proj_hbm, bf16[256,2048]{1,0:T(8,128)(2,1)} %get-tuple-element.42.e1h_hbm, bf16[256,2048]{1,0:T(8,128)(2,1)} %get-tuple-element.43.e1l_hbm, bf16[32,512]{1,0:T(8,128)(2,1)} %get-tuple-element.44.win_hbm, ...), custom_call_target="tpu_custom_call" | custom-call | flops 268435456 | bytes 2330624 | tf_op jit(solution)/shard_map/outgoing/pallas_call | solution.py:95
  124.3 11.2 %all-to-all-done.4.got_ref = f32[16,1,1408]{2,1,0:T(1,128)S(1)} async-done(((f32[16,1,1408]{2,1,0:T(1,128)}), f32[16,1,1408]{2,1,0:T(1,128)S(1)}, u32[]{:S(2)}, u32[]{:S(2)}) %all-to-all-start.4) | async-done | bytes 90144 | tf_op jit(solution)/shard_map/all_to_all | solution.py:700
  135.5 0.7 sum_column.1
Async XLA Ops:
  0.6 24.8 %copy-start.3 = (f32[3,32]{1,0:T(4,128)S(1)}, f32[3,32]{1,0:T(4,128)}, u32[]{:S(2)}) copy-start(f32[3,32]{1,0:T(4,128)} %wout_ref.1) | copy-start | bytes 1156
  0.6 24.8 %copy-start.5 = (f32[32]{0:T(128)S(1)}, f32[32]{0:T(128)}, u32[]{:S(2)}) copy-start(f32[32]{0:T(128)} %param.24) | copy-start | bytes 388
  0.7 24.8 %copy-start.1 = (f32[32,32]{1,0:T(8,128)S(1)}, f32[32,32]{1,0:T(8,128)}, u32[]{:S(2)}) copy-start(f32[32,32]{1,0:T(8,128)} %wmid_ref.1) | copy-start | bytes 12292
  0.7 24.8 %copy-start.4 = (f32[32]{0:T(128)S(1)}, f32[32]{0:T(128)}, u32[]{:S(2)}) copy-start(f32[32]{0:T(128)} %param.22) | copy-start | bytes 388
  0.7 24.8 %copy-start.2 = (f32[32,4]{0,1:T(4,128)S(1)}, f32[32,4]{0,1:T(4,128)}, u32[]{:S(2)}) copy-start(f32[32,4]{0,1:T(4,128)} %param.21) | copy-start | bytes 1540
  6.3 39.8 %all-to-all-start = ((f32[128,1,384]{2,1,0:T(1,128)}), f32[128,1,384]{2,1,0:T(1,128)S(1)}, u32[]{:S(2)}, u32[]{:S(2)}) async-start(f32[128,1,384]{2,1,0:T(1,128)} %get-tuple-element.31), calls=%async_computation | async-start | bytes 393216 | tf_op jit(solution)/shard_map/all_to_all | solution.py:608
  46.1 16.3 %copy-start = (f32[8]{0:T(128)S(1)}, f32[8]{0:T(128)}, u32[]{:S(2)}) copy-start(f32[8]{0:T(128)} %spacing_ref.1) | copy-start | bytes 100
  116.6 18.9 %all-to-all-start.4 = ((f32[16,1,1408]{2,1,0:T(1,128)}), f32[16,1,1408]{2,1,0:T(1,128)S(1)}, u32[]{:S(2)}, u32[]{:S(2)}) async-start(f32[16,1,1408]{2,1,0:T(1,128)} %get-tuple-element.49), calls=%async_computation.4 | async-start | bytes 180224 | tf_op jit(solution)/shard_map/all_to_all | solution.py:700
where the time goes:
time: 137 us; the launch traced here: 136 us
  blocking collectives  50.7 us (37%)
  Pallas kernels  34.1 us (25%)
  waiting for transfers between devices  26.8 us (20%)
  starting transfers between devices  23.8 us (17%)
    pallas_call x8, Pallas kernels, call(): pl.pallas_call(kernel, out_shape=out_shape, in_specs=[space(i, held) for...  34.1 us
    all_to_all x1, blocking collectives, shards(): msg = lax.all_to_all(msg, PLANE, 0, 0)  26.9 us
    all_to_all x1, starting transfers between devices, shards(): msg = lax.all_to_all(msg, PLANE, 0, 0)  19.2 us
    all_to_all x1, waiting for transfers between devices, shards(): msg = lax.all_to_all(msg, PLANE, 0, 0)  15.6 us
    all_to_all x1, blocking collectives, shards(): gathered = lax.all_to_all(gathered, 'x', 0, 0)  12.8 us
    all_to_all x1, waiting for transfers between devices, shards(): totals = lax.all_to_all(totals, COLUMN, 0, 0)  11.2 us
    all_to_all x1, blocking collectives, shards(): totals = lax.all_to_all(totals, SLAB, 0, 0)  11.1 us
    all_to_all x1, starting transfers between devices, shards(): totals = lax.all_to_all(totals, COLUMN, 0, 0)  4.62 us
  transfers between devices with their start and end apart: 2, of which 2 were waited for; matrix products, arithmetic and copies ran while one was open for 0% of the time, Pallas kernels for 6%

commit v1 on v0

v1 whole, which is shorter than its diff:
```python
import functools
import math

import jax
import jax.numpy as jnp
import ml_dtypes
import numpy as np
from jax import lax
from jax.experimental import pallas as pl
from jax.experimental.pallas import tpu as pltpu
from jax.sharding import Mesh
from jax.sharding import PartitionSpec as P

free_surface = 0.05
f32 = jnp.float32
bf16 = jnp.bfloat16
LANES = 128
LEVELS = 8
VMEM_LIMIT = 24 * 1024 * 1024

FINE = (("y", 4), ("zl", 8), ("c", 2), ("zh", 2), ("x", 4))
WIDE = ("y", "zl", "c")
NARROW = ("zh", "x")
PLANE = ("zh", "y", "zl", "c")
SLAB = ("y", "x", "c")
COLUMN = ("zl", "zh")


def dft_table(count, length):
    indices = np.arange(count)
    angle = 2.0 * np.pi / count * (indices[:, None] * indices[None, :] % count)
    return np.concatenate([np.cos(angle), np.sin(angle)], axis=0) * np.sqrt(2.0 / length)


def twiddles(count, length):
    angle = 2.0 * np.pi / length * np.arange(count)[:, None] * np.arange(4)[None, :]
    held = np.zeros((count, LANES))
    held[:, 0:8:2] = np.cos(angle)
    held[:, 1:8:2] = np.sin(angle)
    return held.astype(np.float32)


def wavenumbers(length):
    half = np.arange(length // 2)
    return np.concatenate([half, np.where(half == 0, length // 2, half)])


def two_parts(table):
    high = table.astype(np.float32).astype(ml_dtypes.bfloat16)
    low = (table - high.astype(np.float64)).astype(np.float32).astype(ml_dtypes.bfloat16)
    return np.concatenate([high, low], axis=0)


def eigenvalue(length):
    return -4.0 * np.sin(np.pi / length * wavenumbers(length)) ** 2


def split(value):
    high = value.astype(bf16)
    low = (value - high.astype(f32)).astype(bf16)
    return high, low


def split_f32(value):
    high = value.astype(bf16).astype(f32)
    return high, value - high


def dot(a, b):
    return jnp.dot(a, b, preferred_element_type=f32)


def dot_table(table_ref, b):
    rows = table_ref.shape[0] // 2
    return dot(table_ref[0:rows], b) + dot(table_ref[rows : 2 * rows], b)


def dot_nt(a, b):
    return lax.dot_general(a, b, (((1,), (1,)), ((), ())), preferred_element_type=f32)


def roll(value, shift, axis):
    size = value.shape[axis]
    shift = shift % size
    return value if shift == 0 else pltpu.roll(value, shift, axis)


def lane_of(shape):
    return lax.broadcasted_iota(jnp.int32, shape, len(shape) - 1)


def start_copy(source, target, sems, index):
    copy = pltpu.make_async_copy(source, target, sems.at[index])
    copy.start()
    return copy


def call(kernel, out_shape, args, smem=(), hbm=(), hbm_out=(), scratch=(), flops=0, name=None):
    def space(index, held):
        return pl.BlockSpec(memory_space=held.get(index, pltpu.VMEM))

    held = {i: pltpu.SMEM for i in smem} | {i: pl.ANY for i in hbm}
    args = [
        pltpu.with_memory_space_constraint(a, pltpu.HBM) if i in hbm else a
        for i, a in enumerate(args)
    ]
    moved = sum(int(np.prod(a.shape)) * a.dtype.itemsize for a in args)
    return pl.pallas_call(
        kernel,
        out_shape=out_shape,
        in_specs=[space(i, held) for i in range(len(args))],
        out_specs=[space(i, {o: pl.ANY for o in hbm_out}) for i in range(len(out_shape))],
        scratch_shapes=list(scratch),
        compiler_params=pltpu.CompilerParams(vmem_limit_bytes=VMEM_LIMIT),
        cost_estimate=pl.CostEstimate(flops=flops, bytes_accessed=moved, transcendentals=0),
        name=name,
    )(*args)


def first_row(shape):
    return lax.broadcasted_iota(jnp.int32, shape, 0) == 0


def join(cos_r, sin_r):
    even_c, even_s = cos_r[0] + cos_r[2], sin_r[0] + sin_r[2]
    odd_c, odd_s = cos_r[1] + cos_r[3], sin_r[1] + sin_r[3]
    top = first_row(even_c.shape)
    ends = jnp.where(top, math.sqrt(0.5), 1.0)
    return (
        (even_c + odd_c) * ends,
        cos_r[0] - cos_r[2] - (sin_r[1] - sin_r[3]),
        jnp.where(top, even_c - odd_c, even_s + odd_s) * ends,
        sin_r[0] - sin_r[2] + (cos_r[1] - cos_r[3]),
    )


def part_back(blocks):
    top = first_row(blocks[0].shape)
    ends = jnp.where(top, math.sqrt(0.5), 1.0)
    low_c, high_c, low_s, high_s = blocks
    low_c, low_s = low_c * ends, low_s * ends
    last = jnp.where(top, low_s, 0.0)
    low_s = jnp.where(top, 0.0, low_s)
    even, odd = low_c + last, low_c - last
    return (
        (even + high_c, odd + high_s, even - high_c, odd - high_s),
        (low_s + high_s, low_s - high_c, low_s - high_s, low_s + high_c),
    )


def turn(cos_part, sin_part, cos_turn, sin_turn):
    return cos_part * cos_turn - sin_part * sin_turn, sin_part * cos_turn + cos_part * sin_turn


def turn_of(turn_ref, remainder):
    rows, shape = slice(0, 256), (256, LANES)
    return (
        jnp.broadcast_to(turn_ref[rows, 2 * remainder : 2 * remainder + 1], shape),
        jnp.broadcast_to(turn_ref[rows, 2 * remainder + 1 : 2 * remainder + 2], shape),
    )


def forward_x(cot_hbm, table_hbm, turn_hbm, out_ref, mark_ref,
              table_ref, turn_ref, cot_ref, line_ref, sems):
    first = start_copy(cot_hbm, cot_ref, sems, 0)
    copies = [
        start_copy(table_hbm, table_ref, sems, 1),
        start_copy(turn_hbm, turn_ref, sems, 2),
    ]
    first.wait()
    east, north, up = cot_ref[0, 0], cot_ref[1, 0], cot_ref[2, 0]
    rows, width = east.shape
    east = east - roll(east, -1, 1)
    high, low = split_f32(jnp.concatenate([east, north, up], axis=0))
    none = jnp.zeros((rows, width), f32)
    line_ref[...] = jnp.concatenate([high, none, low, none], axis=0).T
    lines = jnp.concatenate(
        [line_ref[pl.ds(r, 256, stride=4), :].astype(bf16) for r in range(4)], axis=1
    )
    for copy in copies:
        copy.wait()
    got = dot_table(table_ref, lines)
    cos_r, sin_r = [], []
    for r in range(4):
        cos_part = got[0:256, LANES * r : LANES * (r + 1)]
        sin_part = got[256:512, LANES * r : LANES * (r + 1)]
        if r > 0:
            cos_part, sin_part = turn(cos_part, sin_part, *turn_of(turn_ref, r))
        cos_r.append(cos_part)
        sin_r.append(sin_part)
    blocks = [block + roll(block, 64, 1) for block in join(cos_r, sin_r)]
    lane = lane_of((LANES, LANES))
    for field in range(3):
        packed = jnp.zeros((LANES, LANES), f32)
        for t in range(8):
            block = blocks[t // 2][LANES * (t % 2) : LANES * (t % 2 + 1)]
            packed = jnp.where(lane // 16 == t, roll(block, 16 * (t - field), 1), packed)
        out_ref[:, 0, LANES * field : LANES * (field + 1)] = packed
    mark_ref[...] = jnp.zeros(mark_ref.shape, f32)


def pair_turns(turn_ref, pair, within):
    one, two = turn_of(turn_ref, 2 * pair), turn_of(turn_ref, 2 * pair + 1)
    return tuple(jnp.where(within < 8, a, b) for a, b in zip(one, two))


def forward_y(msg_ref, table_hbm, turn_hbm, second_hbm, back_hbm, mark_ref,
              out_ref, turn_ref, second_ref, back_ref, table_ref, sems):
    copies = [
        start_copy(table_hbm, table_ref, sems, 0),
        start_copy(turn_hbm, turn_ref, sems, 1),
    ]
    later_copies = [
        start_copy(back_hbm, back_ref, sems, 2),
        start_copy(second_hbm, second_ref, sems, 3),
    ]
    within = lane_of((64, LANES)) % 16
    highs = []
    lows = []
    for half in range(2):
        part = slice(64 * half, 64 * (half + 1))
        east = msg_ref[part, 0, 0:LANES]
        north = msg_ref[part, 0, LANES : 2 * LANES]
        up = msg_ref[part, 0, 2 * LANES : 3 * LANES]
        after = jnp.where(
            within < 15, roll(north, -1, 1), roll(roll(north, -1, 0), 15, 1)
        )
        for value in (east + north - after, up):
            high, low = split_f32(value)
            highs.append(high)
            lows.append(low)
    shifted = [roll(value, c, 1) for c, value in enumerate(highs + lows)]

    def line_of(j, to):
        line = shifted[0]
        for c in range(1, 8):
            line = jnp.where(within == (c + j) % 16, shifted[c], line)
        return roll(line, to - j, 1)

    lines = []
    for pair in range(2):
        rows = []
        for step in range(4):
            j = 4 * step + 2 * pair
            rows.append(jnp.where(within < 8, line_of(j, 0), line_of(j + 1, 8)).astype(bf16))
        lines.append(jnp.concatenate(rows, axis=0))
    lines = jnp.concatenate(lines, axis=1)
    for copy in copies:
        copy.wait()
    got = dot_table(table_ref, lines)
    within = lane_of((256, LANES)) % 16
    turned = [
        turn(
            got[0:256, LANES * pair : LANES * (pair + 1)],
            got[256:512, LANES * pair : LANES * (pair + 1)],
            *pair_turns(turn_ref, pair, within),
        )
        for pair in range(2)
    ]
    cos_r = [turned[0][0], roll(turned[0][0], -8, 1), turned[1][0], roll(turned[1][0], -8, 1)]
    sin_r = [turned[0][1], roll(turned[0][1], -8, 1), turned[1][1], roll(turned[1][1], -8, 1)]
    packed = jnp.zeros((256, LANES), f32)
    for g, block in enumerate(join(cos_r, sin_r)):
        block = block + roll(block, -4, 1)
        packed = jnp.where(within // 4 == g, roll(block, 4 * g, 1), packed)
    for peer in range(4):
        out_ref[peer] = packed
    for copy in later_copies:
        copy.wait()


def vertical(spacing):
    one = jnp.ones((1, LANES), f32)
    none = jnp.zeros((1, LANES), f32)
    spacing = [one * spacing[k] for k in range(LEVELS)]
    inv_dz = [1.0 / value for value in spacing]
    face = [2.0 / (spacing[k] + spacing[k + 1]) for k in range(LEVELS - 1)] + [none]
    lower = [none] + [inv_dz[k] * face[k - 1] for k in range(1, LEVELS)]
    upper = [inv_dz[k] * face[k] for k in range(LEVELS)]
    base = [-(lower[k] + upper[k]) for k in range(LEVELS)]
    base[-1] = base[-1] - free_surface * inv_dz[-1]
    sub = [none] + upper[:-1]
    sup = lower[1:] + [none]
    keep = [one] * (LEVELS - 1) + [none]
    return inv_dz, face, sub, base, sup, keep


def solve_back(got_ref, turn_ref, table_hbm, cot_hbm, mask_hbm, first_hbm, wide_hbm,
               out_ref, cot_ref, mask_ref, first_ref, wide_ref, table_ref, sems):
    copies = [start_copy(table_hbm, table_ref, sems, 0)]
    later_copies = [
        start_copy(cot_hbm, cot_ref, sems, 1),
        start_copy(mask_hbm, mask_ref, sems, 2),
        start_copy(wide_hbm, wide_ref, sems, 3),
        start_copy(first_hbm, first_ref, sems, 4),
    ]
    at = lax.axis_index("x")
    rows = got_ref.shape[1]
    lam = turn_ref[256 : 256 + rows]
    lane = lane_of((rows, LANES))
    inv_dz, face, sub, base, sup, keep = (
        [turn_ref[512 + 8 * i + k : 513 + 8 * i + k] for k in range(LEVELS)]
        for i in range(6)
    )
    ratios = []
    values = []
    below = None
    for k in range(LEVELS):
        packed = got_ref[k % 4]
        half = k // 4
        flux = roll(packed, -(2 * half + 1), 1) * face[k]
        right = roll(packed, -2 * half, 1) - flux
        if k > 0:
            right = right + below
        below = flux
        diagonal = lam + base[k]
        if k > 0:
            diagonal = diagonal - sub[k] * ratios[-1]
            right = right - sub[k] * values[-1]
        inverse = 1.0 / diagonal
        ratios.append(sup[k] * inverse)
        values.append(right * inverse)
    result = [None] * LEVELS
    result[-1] = values[-1]
    for k in range(LEVELS - 2, -1, -1):
        result[k] = values[k] - ratios[k] * result[k + 1]
    scaled = [result[k] * inv_dz[k] for k in range(LEVELS)] + [jnp.zeros_like(lam)]
    change = [(scaled[k] - scaled[k + 1]) * keep[k] for k in range(LEVELS)]

    def own(items, half):
        value = items[4 * half]
        for x in range(1, 4):
            value = jnp.where(at == x, items[4 * half + x], value)
        return value

    column = lane % 4
    both = own(result, 0)
    both = jnp.where(column == 1, roll(own(change, 0), 1, 1), both)
    both = jnp.where(column == 2, roll(own(result, 1), 2, 1), both)
    both = jnp.where(column == 3, roll(own(change, 1), 3, 1), both)
    for copy in copies:
        copy.wait()
    within = lane % 16
    blocks = []
    for g in range(4):
        block = roll(both, -4 * g, 1)
        blocks.append(jnp.where(within < 8, block, roll(block, 8, 1)))
    cos_r, sin_r = part_back(blocks)
    parts = ([], [])
    for pair in range(2):
        cos_part = jnp.where(within < 8, cos_r[2 * pair], cos_r[2 * pair + 1])
        sin_part = jnp.where(within < 8, sin_r[2 * pair], sin_r[2 * pair + 1])
        cos_turn, sin_turn = pair_turns(turn_ref, pair, within)
        for i, value in enumerate(turn(cos_part, sin_part, cos_turn, -sin_turn)):
            high, low = split_f32(jnp.where(within % 8 < 4, value, 0.0))
            parts[i].append((high + roll(low, 4, 1)).astype(bf16))
    columns = jnp.concatenate([jnp.concatenate(part, axis=1) for part in parts], axis=0)
    got = dot_table(table_ref, columns)
    within = lane_of((64, LANES)) % 16
    packed = [jnp.zeros((64, LANES), f32)] * 4
    for pair in range(2):
        found = got[:, LANES * pair : LANES * (pair + 1)]
        found = found + roll(found, -4, 1)
        for step in range(4):
            for one in range(2):
                j = 4 * step + 2 * pair + one
                moved = roll(found[64 * step : 64 * (step + 1)], j - 8 * one, 1)
                for c in range(4):
                    packed[c] = jnp.where(within == (j + c) % 16, moved, packed[c])
    for half in range(2):
        part = slice(64 * half, 64 * (half + 1))
        pressure = roll(packed[2 * half], -2 * half, 1)
        change_up = roll(packed[2 * half + 1], -(2 * half + 1), 1)
        before = jnp.where(
            within > 0, roll(pressure, 1, 1), roll(roll(pressure, 1, 0), -15, 1)
        )
        out_ref[part, 0, 0:LANES] = pressure
        out_ref[part, 0, LANES : 2 * LANES] = change_up
        out_ref[part, 0, 2 * LANES : 3 * LANES] = before - pressure
    for copy in later_copies:
        copy.wait()


CHUNK = 1024


def unit_rows(shape, axis):
    return lax.broadcasted_iota(jnp.int32, shape, axis) % 8


def same_row(value):
    shape = value.shape
    return jnp.where(unit_rows(shape, 0) == unit_rows(shape, 1), value, 0.0)


def gather(shape, step):
    to = lax.broadcasted_iota(jnp.int32, shape, 1)
    return (lax.broadcasted_iota(jnp.int32, shape, 0) // step == to).astype(f32)


def exact(a, b):
    return jnp.dot(a, b, precision=lax.Precision.HIGHEST, preferred_element_type=f32)


def spread(weight, columns):
    tall, wide = weight.shape
    step = (
        lax.broadcasted_iota(jnp.int32, (wide, columns), 1) // 8
        == lax.broadcasted_iota(jnp.int32, (wide, columns), 0)
    ).astype(f32)
    value = exact(weight, step)
    value = jnp.broadcast_to(value[:, None, :], (tall, 8, columns)).reshape(8 * tall, columns)
    return same_row(value)


def closure_forward(vel_hbm, buoy_hbm, win_ref, bin_ref, wmid_ref, bmid_ref, wout_ref,
                    fixed_hbm, mark_ref, spacing_ref,
                    first_hbm, second_hbm, wide_hbm, turn_hbm, done_ref,
                    first_ref, second_ref, wide_ref, turn_ref, vel_ref, buoy_ref, sems, out_sems):
    copies = [
        start_copy(vel_hbm, vel_ref, sems, 0),
        start_copy(buoy_hbm, buoy_ref, sems, 1),
        start_copy(fixed_hbm, turn_ref, sems, 2),
    ]
    win_t = win_ref[...]
    wmid = wmid_ref[...]
    wout_h, wout_l = split_f32(spread(wout_ref[...].T, 32))
    wide_ref[0:256, 0:96] = jnp.concatenate([wout_h, wout_h, wout_l], axis=1).astype(bf16)
    wide_ref[0:256, 96:128] = jnp.zeros((256, 32), bf16)
    wide_ref[0:256, 128:384], wide_ref[0:256, 384:640] = split(spread(wmid.T, 256))
    wide_ref[256:288, 0:128] = jnp.zeros((32, 128), bf16)
    wide_ref[256:288, 128:384], wide_ref[256:288, 384:640] = split(spread(win_t, 256))
    win_h, win_l = split_f32(spread(win_t.T, 32))
    win_cat = jnp.concatenate([win_h, win_h, win_l], axis=1).astype(bf16)
    wmh, wml = split(spread(wmid, 256))

    def tall(row):
        column = row.T
        return jnp.broadcast_to(column[:, None, :], (32, 8, 1)).reshape(256, 1)

    b_in, b_mid = tall(bin_ref[...]), tall(bmid_ref[...])
    for copy in copies:
        copy.wait()
    own = turn_ref[pl.ds(512 + lax.axis_index(PLANE), 1), :]
    turn_ref[256:512] = turn_ref[256:512] + own
    for i, rows in enumerate(vertical([spacing_ref[k] for k in range(LEVELS)])):
        turn_ref[512 + 8 * i : 520 + 8 * i] = jnp.concatenate(rows, axis=0)
    copies = [
        start_copy(wide_ref, wide_hbm, out_sems, 0),
        start_copy(turn_ref, turn_hbm, out_sems, 1),
    ]
    width = buoy_ref.shape[-1]
    for half in range(2):
        part = slice(8 * half, 8 * (half + 1))
        for start in range(0, width, CHUNK):
            col = slice(start, start + CHUNK)
            to = slice(half * width + start, half * width + start + CHUNK)
            feats = jnp.concatenate(
                [vel_ref[c, 0, part, col] for c in range(3)] + [buoy_ref[0, part, col]], axis=0
            )
            high, low = split_f32(feats)
            stack = jnp.concatenate([high, low, high], axis=0).astype(bf16)
            first_ref[512:608, to] = jnp.concatenate(
                [high, low, jnp.ones((32, CHUNK), f32)], axis=0
            ).astype(bf16)
            first = jnp.tanh(dot(win_cat, stack) + b_in)
            fh, fl = split(first)
            first_ref[0:256, to] = fh
            first_ref[256:512, to] = fl
            second = dot(wmh, fh) + dot(wmh, fl) + dot(wml, fh)
            second = jnp.tanh(second + b_mid)
            sh, sl = split(second)
            second_ref[0:256, to] = sh
            second_ref[256:512, to] = sl
        whole = slice(half * width, (half + 1) * width)
        for i, (held, target) in enumerate(((first_ref, first_hbm), (second_ref, second_hbm))):
            copies.append(
                start_copy(held.at[:, whole], target.at[:, whole], out_sems, 2 + 2 * half + i)
            )
    done_ref[...] = jnp.zeros(done_ref.shape, f32)
    for copy in copies:
        copy.wait()


def closure_back(msg_ref, turn_ref, second_ref, table_ref, cot_ref, mask_ref, first_ref,
                 wide_ref, total_ref, gvel_hbm, gbuoy_hbm,
                 line_ref, e1h_ref, e1l_ref, e2h_ref, e2l_ref, dl_ref, b2_ref,
                 gvel_ref, gbuoy_ref, out_sems):
    width = mask_ref.shape[-1]
    lane = lane_of((LANES, LANES))
    halves = []
    for t in range(8):
        value = jnp.zeros((LANES, LANES), f32)
        for field in range(3):
            item = msg_ref[:, 0, LANES * field : LANES * (field + 1)]
            value = jnp.where(lane // 16 == field, roll(item, 16 * (field - t), 1), value)
        halves.append(value)
    cos_r, sin_r = part_back(
        [jnp.concatenate(halves[2 * i : 2 * i + 2], axis=0) for i in range(4)]
    )
    parts = ([], [])
    for r in range(4):
        pair = (cos_r[r], sin_r[r])
        if r > 0:
            cos_turn, sin_turn = turn_of(turn_ref, r)
            pair = turn(*pair, cos_turn, -sin_turn)
        for i, value in enumerate(pair):
            high, low = split_f32(value)
            parts[i].append((high + roll(low, 64, 1)).astype(bf16))
    columns = jnp.concatenate([jnp.concatenate(part, axis=1) for part in parts], axis=0)
    found = dot_table(table_ref, columns)
    for r in range(4):
        block = found[:, LANES * r : LANES * (r + 1)]
        line_ref[pl.ds(r, 256, stride=4), :] = block + roll(block, 64, 1)
    field = line_ref[...].T
    pressure = field[0:16]
    east_back = roll(pressure, 1, 1) - pressure
    projected = (
        cot_ref[0, 0] - east_back,
        cot_ref[1, 0] - field[32:48],
        cot_ref[2, 0] - field[16:32],
    )
    wet = mask_ref[0].astype(f32)
    out_copies = []
    deltas = [value * wet for value in projected]
    blank = jnp.zeros((8, CHUNK), f32)
    bias2 = jnp.zeros((256, LANES), f32)
    for half in range(2):
        part = slice(8 * half, 8 * (half + 1))
        for start in range(0, width, CHUNK):
            col = slice(start, start + CHUNK)
            to = slice(half * width + start, half * width + start + CHUNK)
            delta = jnp.concatenate([value[part, col] for value in deltas] + [blank], axis=0)
            dh, dl = split_f32(delta)
            stack = jnp.concatenate([dh, dl, dh], axis=0).astype(bf16)
            dl_ref[:, to] = stack[0:64]
            second = second_ref[0:256, to].astype(f32) + second_ref[256:512, to].astype(f32)
            err2 = dot(wide_ref[0:256, 0:96], stack) * (1.0 - second * second)
            bias2 = bias2 + sum(err2[:, LANES * i : LANES * (i + 1)] for i in range(CHUNK // LANES))
            e2h, e2l = split(err2)
            e2h_ref[:, to] = e2h
            e2l_ref[:, to] = e2l
            first = first_ref[0:256, to].astype(f32) + first_ref[256:512, to].astype(f32)
            err1 = (
                dot(wide_ref[0:256, 128:384], e2h)
                + dot(wide_ref[0:256, 128:384], e2l)
                + dot(wide_ref[0:256, 384:640], e2h)
            )
            err1 = err1 * (1.0 - first * first)
            e1h, e1l = split(err1)
            e1h_ref[:, to] = e1h
            e1l_ref[:, to] = e1l
            out = (
                dot(wide_ref[256:288, 128:384], e1h)
                + dot(wide_ref[256:288, 128:384], e1l)
                + dot(wide_ref[256:288, 384:640], e1h)
            )
            for c in range(3):
                gvel_ref[c, 0, part, col] = projected[c][part, col] + out[8 * c : 8 * (c + 1)]
            gbuoy_ref[0, part, col] = out[24:32]
        out_copies += [
            start_copy(gvel_ref.at[:, :, part, :], gvel_hbm.at[:, :, part, :], out_sems, 2 * half),
            start_copy(gbuoy_ref.at[:, part, :], gbuoy_hbm.at[:, part, :], out_sems, 2 * half + 1),
        ]
    b2_ref[...] = bias2
    mid = (
        dot_nt(e2h_ref[...], first_ref[0:256])
        + dot_nt(e2h_ref[...], first_ref[256:512])
        + dot_nt(e2l_ref[...], first_ref[0:256])
    )
    both1 = dot_nt(first_ref[512:608], e1h_ref[...])
    rest1 = dot_nt(first_ref[512:608], e1l_ref[...])
    win = both1[0:32] + both1[32:64] + rest1[0:32]
    bin_ = both1[64:65] + rest1[64:65]
    both2 = dot_nt(dl_ref[...], second_ref[0:256])
    rest2 = dot_nt(dl_ref[...], second_ref[256:512])
    wout = both2[0:32] + both2[32:64] + rest2[0:32]

    def fold_rows(value):
        return jnp.sum(value.reshape(value.shape[0] // 8, 8, value.shape[1]), axis=1)

    to_unit = gather((256, LANES), 8)
    mid = exact(fold_rows(same_row(mid)), to_unit)
    small = [fold_rows(same_row(win)), fold_rows(same_row(wout)), bin_, jnp.zeros((7, 256), f32)]
    small = exact(jnp.concatenate(small, axis=0), to_unit)
    b2 = lax.dot_general(
        jnp.ones((8, LANES), f32),
        fold_rows(b2_ref[...]),
        (((1,), (1,)), ((), ())),
        precision=lax.Precision.HIGHEST,
        preferred_element_type=f32,
    )
    units = jnp.concatenate([mid[8 * i : 8 * (i + 1), 0:32] for i in range(4)], axis=1)
    rows = [units[i : i + 1] for i in range(8)]
    rows.append(jnp.concatenate([small[i : i + 1, 0:32] for i in range(4)], axis=1))
    rows.append(
        jnp.concatenate([small[i : i + 1, 0:32] for i in range(4, 7)] + [b2[0:1]], axis=1)
    )
    rows.append(small[8:9])
    for peer in range(32):
        for i, row in enumerate(rows):
            total_ref[peer, :, LANES * i : LANES * (i + 1)] = row
    for copy in out_copies:
        copy.wait()


def sum_slab(got_ref, out_ref):
    total = jnp.sum(got_ref[...], axis=0)
    for peer in range(16):
        out_ref[peer] = total


def sum_column(scale, got_ref, win_ref, bin_ref, wmid_ref, bmid_ref, wout_ref):
    total = jnp.sum(got_ref[...], axis=0) * scale
    rows = [total[:, LANES * i : LANES * (i + 1)] for i in range(11)]
    units = jnp.concatenate(rows[:8], axis=0)
    wmid_ref[...] = jnp.concatenate([units[:, 32 * i : 32 * (i + 1)] for i in range(4)], axis=0)
    win_ref[...] = jnp.concatenate([rows[8][:, 32 * i : 32 * (i + 1)] for i in range(4)], axis=0)
    wout_ref[...] = jnp.concatenate([rows[9][:, 32 * i : 32 * (i + 1)] for i in range(3)], axis=0)
    bmid_ref[...] = rows[9][:, 96:128]
    bin_ref[...] = rows[10][:, 0:32]


def shards(velocity, buoyancy, cell_mask, spacing, cotangent, w_in, b_in, w_mid, b_mid, w_out):
    levels, rows, width = buoyancy.shape
    depth = spacing.shape[0]
    span_y = rows * 64
    table = dft_table(256, 1024)
    table_y = table[:, (np.arange(256) % 64) * 4 + np.arange(256) // 64]
    x_table, y_table, x_back, y_back = (
        jnp.asarray(two_parts(item)) for item in (table, table_y, table.T, table_y.T)
    )
    eigen = eigenvalue(width)
    lanes = np.arange(LANES)
    ey = eigen.reshape(4, 256)[lanes % 16 // 4].T.astype(np.float32)
    ex = eigen[np.arange(128)[:, None] + 128 * (lanes[None, :] // 16)].astype(np.float32)
    turns = twiddles(256, 1024)
    fixed = jnp.asarray(np.concatenate([turns, ey, ex], axis=0))
    turns = jnp.asarray(turns)
    cells = rows * width // 8
    dma = pltpu.SemaphoreType.DMA
    type_of = jax.ShapeDtypeStruct
    table = pltpu.VMEM((1024, 256), bf16)
    back_table = pltpu.VMEM((512, 512), bf16)
    turn_held = pltpu.VMEM((640, LANES), f32)
    first_held = pltpu.VMEM((608, cells), bf16)
    second_held = pltpu.VMEM((512, cells), bf16)
    wide = pltpu.VMEM((256, cells), bf16)
    wide_held = pltpu.VMEM((288, 640), bf16)
    mark_type = type_of((8, LANES), f32)
    table_flops = 4 * 512 * 256 * 512
    msg_type = type_of((128, 1, 3 * LANES), f32)
    msg, mark = call(
        forward_x,
        (msg_type, mark_type),
        (cotangent, x_table, turns),
        hbm=(0, 1, 2),
        scratch=(
            table,
            pltpu.VMEM((256, LANES), f32),
            pltpu.VMEM(cotangent.shape, f32),
            pltpu.VMEM((1024, LANES), f32),
            dma((3,)),
        ),
        flops=table_flops,
        name="forward_x",
    )
    msg = lax.all_to_all(msg, PLANE, 0, 0)

    first, second, weights, turns, mark = call(
        closure_forward,
        (
            pltpu.HBM((608, cells), bf16),
            pltpu.HBM((512, cells), bf16),
            pltpu.HBM((288, 640), bf16),
            pltpu.HBM((640, LANES), f32),
            mark_type,
        ),
        (velocity, buoyancy, w_in.T, b_in[None], w_mid, b_mid[None], w_out, fixed, mark, spacing),
        hbm=(0, 1, 7),
        smem=(9,),
        hbm_out=range(4),
        scratch=(
            first_held,
            second_held,
            wide_held,
            turn_held,
            pltpu.VMEM(velocity.shape, f32),
            pltpu.VMEM(buoyancy.shape, f32),
            dma((3,)),
            dma((6,)),
        ),
        flops=2 * 256 * 256 * cells * 4,
        name="closure_forward",
    )
    gathered, turns, second, x_back = call(
        forward_y,
        (type_of((4, 256, LANES), f32), turn_held, second_held, back_table),
        (msg, y_table, turns, second, x_back, mark),
        hbm=range(1, 5),
        scratch=(table, dma((4,))),
        flops=table_flops,
        name="forward_y",
    )
    gathered = lax.all_to_all(gathered, "x", 0, 0)
    msg, cotangent, cell_mask, first, weights = call(
        solve_back,
        (
            msg_type,
            pltpu.VMEM(cotangent.shape, f32),
            pltpu.VMEM(cell_mask.shape, jnp.int32),
            first_held,
            wide_held,
        ),
        (gathered, turns, y_back, cotangent, cell_mask, first, weights),
        hbm=range(2, 7),
        scratch=(back_table, dma((5,))),
        flops=table_flops,
        name="solve_back",
    )
    msg = lax.all_to_all(msg, PLANE, 0, 0)
    totals, grad_velocity, grad_buoyancy = call(
        closure_back,
        (
            type_of((32, 1, 11 * LANES), f32),
            pltpu.HBM(cotangent.shape, f32),
            pltpu.HBM(buoyancy.shape, f32),
        ),
        (msg, turns, second, x_back, cotangent, cell_mask, first, weights),
        hbm_out=(1, 2),
        scratch=(
            pltpu.VMEM((1024, LANES), f32),
            wide,
            wide,
            wide,
            wide,
            pltpu.VMEM((64, cells), bf16),
            pltpu.VMEM((256, LANES), f32),
            pltpu.VMEM(cotangent.shape, f32),
            pltpu.VMEM(buoyancy.shape, f32),
            dma((4,)),
        ),
        flops=table_flops + 2 * 256 * 256 * cells * 10,
        name="closure_back",
    )
    totals = lax.all_to_all(totals, SLAB, 0, 0)
    (totals,) = call(sum_slab, (type_of((16, 1, 11 * LANES), f32),), (totals,), name="sum_slab")
    totals = lax.all_to_all(totals, COLUMN, 0, 0)
    scale = 1.0 / math.sqrt(width * span_y * depth)
    grad_in, grad_b_in, grad_mid, grad_b_mid, grad_out = call(
        functools.partial(sum_column, scale),
        (
            type_of((4, 32), f32),
            type_of((1, 32), f32),
            type_of((32, 32), f32),
            type_of((1, 32), f32),
            type_of((3, 32), f32),
        ),
        (totals,),
        name="sum_column",
    )
    return (
        grad_velocity,
        grad_buoyancy,
        grad_in.T,
        grad_b_in[0],
        grad_mid,
        grad_b_mid[0],
        grad_out,
    )


def solution(mesh):
    fine = Mesh(
        mesh.devices.reshape([size for _, size in FINE]), tuple(name for name, _ in FINE)
    )
    field = P(None, NARROW, WIDE, None)
    cell = P(NARROW, WIDE, None)
    in_specs = (field, cell, cell, P(), field, P(), P(), P(), P(), P())
    out_specs = (field, cell, P(), P(), P(), P(), P())
    return jax.shard_map(shards, mesh=fine, in_specs=in_specs, out_specs=out_specs, check_vma=False)
```

time: 137 us -> 125 us (0.912)
  blocking collectives: 50.7 us -> 68.5 us
  waiting for transfers between devices: 26.8 us -> 11.2 us
  Pallas kernels: 34.1 us -> 20.8 us
  starting transfers between devices: 23.8 us -> 19.2 us
  local copies, waits for them, and re-layouts: 0.02 us -> 4.04 us
    all_to_all x0 -> x1, blocking collectives: none -> 18 us  [shards(): totals = lax.all_to_all(totals, COLUMN, 0, 0)]
    pallas_call x8 -> x7, Pallas kernels: 34.1 us -> 20.8 us  [call(): pl.pallas_call(kernel, out_shape=out_shape, in_specs=[space(i, held) for...]
    all_to_all x1 -> x0, waiting for transfers between devices: 11.2 us -> none  [shards(): totals = lax.all_to_all(totals, COLUMN, 0, 0)]
    all_to_all x1 -> x0, starting transfers between devices: 4.62 us -> none  [shards(): totals = lax.all_to_all(totals, COLUMN, 0, 0)]
    all_to_all x1, waiting for transfers between devices: 15.6 us -> 11.2 us  [shards(): msg = lax.all_to_all(msg, PLANE, 0, 0)]
    unnamed x12, local copies, waits for them, and re-layouts: 0.02 us -> 4.04 us
  transfers between devices with their start and end apart: 2 -> 1, of which waited for: 2 -> 1; matrix products, arithmetic and copies ran while one was open for 0% -> 0% of each run, Pallas kernels for 6% -> 4%
where the time goes in v1:
time: 125 us; the launch traced here: 124 us
  blocking collectives  68.5 us (55%)
  Pallas kernels  20.8 us (17%)
  starting transfers between devices  19.2 us (15%)
  waiting for transfers between devices  11.2 us (9%)
  local copies, waits for them, and re-layouts  4.04 us (3%)
    all_to_all x1, blocking collectives, shards(): msg = lax.all_to_all(msg, PLANE, 0, 0)  26.7 us
    pallas_call x7, Pallas kernels, call(): pl.pallas_call(kernel, out_shape=out_shape, in_specs=[space(i, held) for...  20.8 us
    all_to_all x1, starting transfers between devices, shards(): msg = lax.all_to_all(msg, PLANE, 0, 0)  19.2 us
    all_to_all x1, blocking collectives, shards(): totals = lax.all_to_all(totals, COLUMN, 0, 0)  18 us
    all_to_all x1, blocking collectives, shards(): gathered = lax.all_to_all(gathered, 'x', 0, 0)  12.8 us
    all_to_all x1, waiting for transfers between devices, shards(): msg = lax.all_to_all(msg, PLANE, 0, 0)  11.2 us
    all_to_all x1, blocking collectives, shards(): totals = lax.all_to_all(totals, SLAB, 0, 0)  11.1 us
    unnamed x12, local copies, waits for them, and re-layouts  4.04 us
  transfers between devices with their start and end apart: 1, of which 1 were waited for; matrix products, arithmetic and copies ran while one was open for 0% of the time, Pallas kernels for 4%

profile of v1, /device:TPU:32, one launch (start us, length us, event | category | flops | bytes accessed | tf_op | source)
XLA Modules:
  0.0 124.5 jit_solution(17999295881908260109)
XLA Ops:
  0.6 3.0 %forward_x.1 = (f32[128,1,384]{2,1,0:T(1,128)}, f32[8,128]{1,0:T(8,128)S(1)}) custom-call(f32[3,1,16,1024]{3,2,1,0:T(8,128)} %cot_hbm.3, bf16[1024,256]{1,0:T(8,128)(2,1)} %constant.12.clone.table_hbm, f32[256,128]{1,0:T(8,128)} %constant.17.clone.turn_hbm), custom_call_target="tpu_custom_call" | custom-call | flops 268435456 | bytes 851968 | tf_op jit(solution)/shard_map/forward_x/pallas_call | solution.py:108
  3.7 19.2 %all-to-all-start = ((f32[128,1,384]{2,1,0:T(1,128)}), f32[128,1,384]{2,1,0:T(1,128)S(1)}, u32[]{:S(2)}, u32[]{:S(2)}) async-start(f32[128,1,384]{2,1,0:T(1,128)} %get-tuple-element.31), calls=%async_computation | async-start | bytes 393216 | tf_op jit(solution)/shard_map/all_to_all | solution.py:668
  22.8 0.0 copy-start
  22.9 0.7 copy-done
  23.6 0.0 copy-start.1
  23.6 0.7 copy-done.1
  24.2 0.0 copy-start.2
  24.2 0.7 copy-done.2
  24.9 0.0 copy-start.3
  24.9 0.7 copy-done.3
  25.6 0.0 copy-start.4
  25.6 0.7 copy-done.4
  26.2 0.0 copy-start.5
  26.2 0.7 copy-done.5
  26.9 5.4 %closure_forward.1 = (bf16[608,2048]{1,0:T(8,128)(2,1)}, bf16[512,2048]{1,0:T(8,128)(2,1)}, bf16[288,640]{1,0:T(8,128)(2,1)}, f32[640,128]{1,0:T(8,128)}, f32[8,128]{1,0:T(8,128)S(1)}) custom-call(f32[3,1,16,1024]{3,2,1,0:T(8,128)} %vel_hbm.1, f32[1,16,1024]{2,1,0:T(8,128)} %buoy_hbm.1, f32[4,32]{1,0:T(4,128)S(1)} %bitcast.6, f32[1,32]{1,0:T(1,128)S(1)} %bitcast.7, ...), custom_call_target="tpu_custom_call" | custom-call | flops 1073741824 | bytes 599200 | tf_op jit(solution)/shard_map/closure_forward/pallas_call | solution.py:108
  32.3 11.2 %all-to-all-done.msg_ref = f32[128,1,384]{2,1,0:T(1,128)S(1)} async-done(((f32[128,1,384]{2,1,0:T(1,128)}), f32[128,1,384]{2,1,0:T(1,128)S(1)}, u32[]{:S(2)}, u32[]{:S(2)}) %all-to-all-start) | async-done | bytes 196640 | tf_op jit(solution)/shard_map/all_to_all | solution.py:668
  43.5 2.2 %forward_y.1 = (f32[4,256,128]{2,1,0:T(8,128)S(1)}, f32[640,128]{1,0:T(8,128)S(1)}, bf16[512,2048]{1,0:T(8,128)(2,1)S(1)}, bf16[512,512]{1,0:T(8,128)(2,1)S(1)}) custom-call(f32[128,1,384]{2,1,0:T(1,128)S(1)} %all-to-all-done.msg_ref, bf16[1024,256]{1,0:T(8,128)(2,1)} %constant.13.clone.table_hbm, f32[640,128]{1,0:T(8,128)} %get-tuple-element.33.turn_hbm, ...), custom_call_target="tpu_custom_call" | custom-call | flops 268435456 | bytes 3674112 | tf_op jit(solution)/shard_map/forward_y/pallas_call | solution.py:108
  45.7 12.8 %all_to_all.25.got_ref = f32[4,256,128]{2,1,0:T(8,128)S(1)} all-to-all(f32[4,256,128]{2,1,0:T(8,128)S(1)} %get-tuple-element.36), channel_id=1, replica_groups=mesh['y'=4,'zl'=8,'c'=2,'zh'=2,'x'=4] {'x'}, dimensions={0} | all-to-all | bytes 1048576 | tf_op jit(solution)/shard_map/all_to_all | solution.py:705
  58.4 2.8 %solve_back.1 = (f32[128,1,384]{2,1,0:T(1,128)S(1)}, f32[3,1,16,1024]{3,2,1,0:T(8,128)S(1)}, s32[1,16,1024]{2,1,0:T(8,128)S(1)}, bf16[608,2048]{1,0:T(8,128)(2,1)S(1)}, bf16[288,640]{1,0:T(8,128)(2,1)S(1)}) custom-call(f32[4,256,128]{2,1,0:T(8,128)S(1)} %all_to_all.25.got_ref, f32[640,128]{1,0:T(8,128)S(1)} %get-tuple-element.37.turn_ref, ...), custom_call_target="tpu_custom_call" | custom-call | flops 268435456 | bytes 4497408 | tf_op jit(solution)/shard_map/solve_back/pallas_call | solution.py:108
  61.3 26.7 %all_to_all.26.msg_ref = f32[128,1,384]{2,1,0:T(1,128)S(1)} all-to-all(f32[128,1,384]{2,1,0:T(1,128)S(1)} %get-tuple-element.40), channel_id=1, replica_groups=mesh['y'=4,'zl'=8,'c'=2,'zh'=2,'x'=4] {'zh','y','zl','c'}, dimensions={0} | all-to-all | bytes 393216 | tf_op jit(solution)/shard_map/all_to_all | solution.py:721
  88.0 6.6 %closure_back.1 = (f32[32,1,1408]{2,1,0:T(1,128)S(1)}, f32[3,1,16,1024]{3,2,1,0:T(8,128)}, f32[1,16,1024]{2,1,0:T(8,128)}) custom-call(f32[128,1,384]{2,1,0:T(1,128)S(1)} %all_to_all.26.msg_ref, f32[640,128]{1,0:T(8,128)S(1)} %get-tuple-element.37.turn_ref, bf16[512,2048]{1,0:T(8,128)(2,1)S(1)} %get-tuple-element.41.second_ref, ...), custom_call_target="tpu_custom_call" | custom-call | flops 2952790016 | bytes 6266880 | tf_op jit(solution)/shard_map/closure_back/pallas_call | solution.py:108
  94.5 11.1 %all_to_all.27.got_ref = f32[32,1,1408]{2,1,0:T(1,128)S(1)} all-to-all(f32[32,1,1408]{2,1,0:T(1,128)S(1)} %get-tuple-element.49), channel_id=1, replica_groups=mesh['y'=4,'zl'=8,'c'=2,'zh'=2,'x'=4] {'y','x','c'}, dimensions={0} | all-to-all | bytes 360448 | tf_op jit(solution)/shard_map/all_to_all | solution.py:746
  105.6 0.1 sum_slab.1
  105.7 18.0 %all_to_all.28.got_ref = f32[16,1,1408]{2,1,0:T(1,128)S(1)} all-to-all(f32[16,1,1408]{2,1,0:T(1,128)S(1)} %sum_slab.1), channel_id=1, replica_groups=mesh['y'=4,'zl'=8,'c'=2,'zh'=2,'x'=4] {'zl','zh'}, dimensions={0} | all-to-all | bytes 180224 | tf_op jit(solution)/shard_map/all_to_all | solution.py:748
  123.7 0.7 sum_column.1
Async XLA Ops:
  3.7 39.8 %all-to-all-start = ((f32[128,1,384]{2,1,0:T(1,128)}), f32[128,1,384]{2,1,0:T(1,128)S(1)}, u32[]{:S(2)}, u32[]{:S(2)}) async-start(f32[128,1,384]{2,1,0:T(1,128)} %get-tuple-element.31), calls=%async_computation | async-start | bytes 393216 | tf_op jit(solution)/shard_map/all_to_all | solution.py:668
  22.8 0.7 copy-start
  23.6 0.7 copy-start.1
  24.2 0.7 copy-start.2
  24.9 0.7 copy-start.3
  25.6 0.7 copy-start.4
  26.2 0.7 copy-start.5

commit v2 on v1

--- a/solution.py
+++ b/solution.py
@@ -195,7 +195,7 @@
         for t in range(8):
             block = blocks[t // 2][LANES * (t % 2) : LANES * (t % 2 + 1)]
             packed = jnp.where(lane // 16 == t, roll(block, 16 * (t - field), 1), packed)
-        out_ref[:, 0, LANES * field : LANES * (field + 1)] = packed
+        out_ref[pl.ds(field, LANES, stride=3), :] = packed
     mark_ref[...] = jnp.zeros(mark_ref.shape, f32)
 
 
@@ -218,10 +218,9 @@
     highs = []
     lows = []
     for half in range(2):
-        part = slice(64 * half, 64 * (half + 1))
-        east = msg_ref[part, 0, 0:LANES]
-        north = msg_ref[part, 0, LANES : 2 * LANES]
-        up = msg_ref[part, 0, 2 * LANES : 3 * LANES]
+        east, north, up = (
+            msg_ref[pl.ds(192 * half + field, 64, stride=3), :] for field in range(3)
+        )
         after = jnp.where(
             within < 15, roll(north, -1, 1), roll(roll(north, -1, 0), 15, 1)
         )
@@ -368,15 +367,13 @@
                 for c in range(4):
                     packed[c] = jnp.where(within == (j + c) % 16, moved, packed[c])
     for half in range(2):
-        part = slice(64 * half, 64 * (half + 1))
         pressure = roll(packed[2 * half], -2 * half, 1)
         change_up = roll(packed[2 * half + 1], -(2 * half + 1), 1)
         before = jnp.where(
             within > 0, roll(pressure, 1, 1), roll(roll(pressure, 1, 0), -15, 1)
         )
-        out_ref[part, 0, 0:LANES] = pressure
-        out_ref[part, 0, LANES : 2 * LANES] = change_up
-        out_ref[part, 0, 2 * LANES : 3 * LANES] = before - pressure
+        for field, value in enumerate((pressure, change_up, before - pressure)):
+            out_ref[pl.ds(192 * half + field, 64, stride=3), :] = value
     for copy in later_copies:
         copy.wait()
 
@@ -413,15 +410,18 @@
     return same_row(value)
 
 
-def closure_forward(vel_hbm, buoy_hbm, win_ref, bin_ref, wmid_ref, bmid_ref, wout_ref,
-                    fixed_hbm, mark_ref, spacing_ref,
+def closure_forward(win_hbm, bin_hbm, wmid_hbm, bmid_hbm, wout_hbm, spacing_hbm,
+                    vel_hbm, buoy_hbm, fixed_hbm, mark_ref,
                     first_hbm, second_hbm, wide_hbm, turn_hbm, done_ref,
-                    first_ref, second_ref, wide_ref, turn_ref, vel_ref, buoy_ref, sems, out_sems):
-    copies = [
-        start_copy(vel_hbm, vel_ref, sems, 0),
-        start_copy(buoy_hbm, buoy_ref, sems, 1),
-        start_copy(fixed_hbm, turn_ref, sems, 2),
-    ]
+                    win_ref, bin_ref, wmid_ref, bmid_ref, wout_ref, spacing_ref,
+                    vel_ref, buoy_ref, turn_ref, first_ref, second_ref, wide_ref, sems, out_sems):
+    sources = (win_hbm, bin_hbm, wmid_hbm, bmid_hbm, wout_hbm, spacing_hbm)
+    sources += (vel_hbm, buoy_hbm, fixed_hbm)
+    targets = (win_ref, bin_ref, wmid_ref, bmid_ref, wout_ref, spacing_ref)
+    targets += (vel_ref, buoy_ref, turn_ref)
+    copies = [start_copy(*pair, sems, i) for i, pair in enumerate(zip(sources, targets))]
+    for copy in copies[:6]:
+        copy.wait()
     win_t = win_ref[...]
     wmid = wmid_ref[...]
     wout_h, wout_l = split_f32(spread(wout_ref[...].T, 32))
@@ -439,11 +439,11 @@
         return jnp.broadcast_to(column[:, None, :], (32, 8, 1)).reshape(256, 1)
 
     b_in, b_mid = tall(bin_ref[...]), tall(bmid_ref[...])
-    for copy in copies:
+    for copy in copies[6:]:
         copy.wait()
     own = turn_ref[pl.ds(512 + lax.axis_index(PLANE), 1), :]
     turn_ref[256:512] = turn_ref[256:512] + own
-    for i, rows in enumerate(vertical([spacing_ref[k] for k in range(LEVELS)])):
+    for i, rows in enumerate(vertical([spacing_ref[:, k : k + 1] for k in range(LEVELS)])):
         turn_ref[512 + 8 * i : 520 + 8 * i] = jnp.concatenate(rows, axis=0)
     copies = [
         start_copy(wide_ref, wide_hbm, out_sems, 0),
@@ -489,10 +489,10 @@
     width = mask_ref.shape[-1]
     lane = lane_of((LANES, LANES))
     halves = []
+    items = [msg_ref[pl.ds(field, LANES, stride=3), :] for field in range(3)]
     for t in range(8):
         value = jnp.zeros((LANES, LANES), f32)
-        for field in range(3):
-            item = msg_ref[:, 0, LANES * field : LANES * (field + 1)]
+        for field, item in enumerate(items):
             value = jnp.where(lane // 16 == field, roll(item, 16 * (field - t), 1), value)
         halves.append(value)
     cos_r, sin_r = part_back(
@@ -597,28 +597,40 @@
         jnp.concatenate([small[i : i + 1, 0:32] for i in range(4, 7)] + [b2[0:1]], axis=1)
     )
     rows.append(small[8:9])
+    rows = jnp.concatenate(rows, axis=0)
     for peer in range(32):
-        for i, row in enumerate(rows):
-            total_ref[peer, :, LANES * i : LANES * (i + 1)] = row
+        total_ref[11 * peer : 11 * (peer + 1), :] = rows
     for copy in out_copies:
         copy.wait()
 
 
+def sum_rows(got_ref):
+    return [
+        jnp.sum(got_ref[pl.ds(i, got_ref.shape[0] // 11, stride=11), :], axis=0, keepdims=True)
+        for i in range(11)
+    ]
+
+
 def sum_slab(got_ref, out_ref):
-    total = jnp.sum(got_ref[...], axis=0)
+    total = jnp.concatenate(sum_rows(got_ref), axis=0)
     for peer in range(16):
-        out_ref[peer] = total
+        out_ref[11 * peer : 11 * (peer + 1), :] = total
 
 
 def sum_column(scale, got_ref, win_ref, bin_ref, wmid_ref, bmid_ref, wout_ref):
-    total = jnp.sum(got_ref[...], axis=0) * scale
-    rows = [total[:, LANES * i : LANES * (i + 1)] for i in range(11)]
+    rows = [row * scale for row in sum_rows(got_ref)]
     units = jnp.concatenate(rows[:8], axis=0)
     wmid_ref[...] = jnp.concatenate([units[:, 32 * i : 32 * (i + 1)] for i in range(4)], axis=0)
     win_ref[...] = jnp.concatenate([rows[8][:, 32 * i : 32 * (i + 1)] for i in range(4)], axis=0)
     wout_ref[...] = jnp.concatenate([rows[9][:, 32 * i : 32 * (i + 1)] for i in range(3)], axis=0)
     bmid_ref[...] = rows[9][:, 96:128]
     bin_ref[...] = rows[10][:, 0:32]
+
+
+def trade(rows, peers, axes):
+    size = rows.shape[0] // peers * LANES
+    got = lax.all_to_all(rows.reshape(peers, 1, size), axes, 0, 0)
+    return got.reshape(rows.shape)
 
 
 def shards(velocity, buoyancy, cell_mask, spacing, cotangent, w_in, b_in, w_mid, b_mid, w_out):
@@ -649,7 +661,7 @@
     wide_held = pltpu.VMEM((288, 640), bf16)
     mark_type = type_of((8, LANES), f32)
     table_flops = 4 * 512 * 256 * 512
-    msg_type = type_of((128, 1, 3 * LANES), f32)
+    msg_type = type_of((128 * 3, LANES), f32)
     msg, mark = call(
         forward_x,
         (msg_type, mark_type),
@@ -665,7 +677,7 @@
         flops=table_flops,
         name="forward_x",
     )
-    msg = lax.all_to_all(msg, PLANE, 0, 0)
+    msg = trade(msg, 128, PLANE)
 
     first, second, weights, turns, mark = call(
         closure_forward,
@@ -676,18 +688,24 @@
             pltpu.HBM((640, LANES), f32),
             mark_type,
         ),
-        (velocity, buoyancy, w_in.T, b_in[None], w_mid, b_mid[None], w_out, fixed, mark, spacing),
-        hbm=(0, 1, 7),
-        smem=(9,),
+        (w_in.T, b_in[None], w_mid, b_mid[None], w_out, spacing[None])
+        + (velocity, buoyancy, fixed, mark),
+        hbm=range(9),
         hbm_out=range(4),
         scratch=(
+            pltpu.VMEM((4, 32), f32),
+            pltpu.VMEM((1, 32), f32),
+            pltpu.VMEM((32, 32), f32),
+            pltpu.VMEM((1, 32), f32),
+            pltpu.VMEM((3, 32), f32),
+            pltpu.VMEM((1, LEVELS), f32),
+            pltpu.VMEM(velocity.shape, f32),
+            pltpu.VMEM(buoyancy.shape, f32),
+            turn_held,
             first_held,
             second_held,
             wide_held,
-            turn_held,
-            pltpu.VMEM(velocity.shape, f32),
-            pltpu.VMEM(buoyancy.shape, f32),
-            dma((3,)),
+            dma((9,)),
             dma((6,)),
         ),
         flops=2 * 256 * 256 * cells * 4,
@@ -718,11 +736,11 @@
         flops=table_flops,
         name="solve_back",
     )
-    msg = lax.all_to_all(msg, PLANE, 0, 0)
+    msg = trade(msg, 128, PLANE)
     totals, grad_velocity, grad_buoyancy = call(
         closure_back,
         (
-            type_of((32, 1, 11 * LANES), f32),
+            type_of((32 * 11, LANES), f32),
             pltpu.HBM(cotangent.shape, f32),
             pltpu.HBM(buoyancy.shape, f32),
         ),
@@ -743,9 +761,9 @@
         flops=table_flops + 2 * 256 * 256 * cells * 10,
         name="closure_back",
     )
-    totals = lax.all_to_all(totals, SLAB, 0, 0)
-    (totals,) = call(sum_slab, (type_of((16, 1, 11 * LANES), f32),), (totals,), name="sum_slab")
-    totals = lax.all_to_all(totals, COLUMN, 0, 0)
+    totals = trade(totals, 32, SLAB)
+    (totals,) = call(sum_slab, (type_of((16 * 11, LANES), f32),), (totals,), name="sum_slab")
+    totals = trade(totals, 16, COLUMN)
     scale = 1.0 / math.sqrt(width * span_y * depth)
     grad_in, grad_b_in, grad_mid, grad_b_mid, grad_out = call(
         functools.partial(sum_column, scale),

time: 125 us -> 125 us (level)
  waiting for transfers between devices: 11.2 us -> 16.1 us
  local copies, waits for them, and re-layouts: 4.04 us -> 0 us
    all_to_all x1, waiting for transfers between devices: 11.2 us -> 16.1 us  [trade(): got = lax.all_to_all(rows.reshape(peers, 1, size), axes, 0, 0)]
    unnamed x12 -> x0, local copies, waits for them, and re-layouts: 4.04 us -> none
where the time goes in v2:
time: 125 us; the launch traced here: 124 us
  blocking collectives  68.5 us (55%)
  Pallas kernels  19.7 us (16%)
  starting transfers between devices  19.2 us (15%)
  waiting for transfers between devices  16.1 us (13%)
    all_to_all x3, blocking collectives, trade(): got = lax.all_to_all(rows.reshape(peers, 1, size), axes, 0, 0)  55.7 us
    pallas_call x7, Pallas kernels, call(): pl.pallas_call(kernel, out_shape=out_shape, in_specs=[space(i, held) for...  19.7 us
    all_to_all x1, starting transfers between devices, trade(): got = lax.all_to_all(rows.reshape(peers, 1, size), axes, 0, 0)  19.2 us
    all_to_all x1, waiting for transfers between devices, trade(): got = lax.all_to_all(rows.reshape(peers, 1, size), axes, 0, 0)  16.1 us
    all_to_all x1, blocking collectives, shards(): gathered = lax.all_to_all(gathered, 'x', 0, 0)  12.8 us
  transfers between devices with their start and end apart: 1, of which 1 were waited for; matrix products, arithmetic and copies ran while one was open for 0% of the time, Pallas kernels for 4%

profile of v2, /device:TPU:32, one launch (start us, length us, event | category | flops | bytes accessed | tf_op | source)
XLA Modules:
  0.0 124.2 jit_solution(6826164691855373780)
XLA Ops:
  0.6 3.0 %forward_x.1 = (f32[384,128]{1,0:T(8,128)}, f32[8,128]{1,0:T(8,128)S(1)}) custom-call(f32[3,1,16,1024]{3,2,1,0:T(8,128)} %cot_hbm.3, bf16[1024,256]{1,0:T(8,128)(2,1)} %constant.12.clone.table_hbm, f32[256,128]{1,0:T(8,128)} %constant.17.clone.turn_hbm), custom_call_target="tpu_custom_call" | custom-call | flops 268435456 | bytes 851968 | tf_op jit(solution)/shard_map/forward_x/pallas_call | solution.py:108
  3.6 19.2 %all-to-all-start = ((f32[128,1,384]{2,1,0:T(1,128)}), f32[128,1,384]{2,1,0:T(1,128)S(1)}, u32[]{:S(2)}, u32[]{:S(2)}) async-start(f32[128,1,384]{2,1,0:T(1,128)} %bitcast), calls=%async_computation | async-start | bytes 393216 | tf_op jit(solution)/shard_map/all_to_all | solution.py:632
  22.8 4.6 %closure_forward.1 = (bf16[608,2048]{1,0:T(8,128)(2,1)}, bf16[512,2048]{1,0:T(8,128)(2,1)}, bf16[288,640]{1,0:T(8,128)(2,1)}, f32[640,128]{1,0:T(8,128)}, f32[8,128]{1,0:T(8,128)S(1)}) custom-call(f32[4,32]{1,0:T(4,128)} %bitcast.22, f32[1,32]{1,0:T(1,128)} %bitcast.24, f32[32,32]{1,0:T(8,128)} %wmid_hbm.1, f32[1,32]{1,0:T(1,128)} %bitcast.25, ...), custom_call_target="tpu_custom_call" | custom-call | flops 1073741824 | bytes 599200 | tf_op jit(solution)/shard_map/closure_forward/pallas_call | solution.py:108
  27.4 16.1 %all-to-all-done = f32[128,1,384]{2,1,0:T(1,128)S(1)} async-done(((f32[128,1,384]{2,1,0:T(1,128)}), f32[128,1,384]{2,1,0:T(1,128)S(1)}, u32[]{:S(2)}, u32[]{:S(2)}) %all-to-all-start) | async-done | bytes 196640 | tf_op jit(solution)/shard_map/all_to_all | solution.py:632
  43.5 2.1 %forward_y.1 = (f32[4,256,128]{2,1,0:T(8,128)S(1)}, f32[640,128]{1,0:T(8,128)S(1)}, bf16[512,2048]{1,0:T(8,128)(2,1)S(1)}, bf16[512,512]{1,0:T(8,128)(2,1)S(1)}) custom-call(f32[384,128]{1,0:T(8,128)S(1)} %bitcast.15, bf16[1024,256]{1,0:T(8,128)(2,1)} %constant.13.clone.table_hbm, f32[640,128]{1,0:T(8,128)} %get-tuple-element.33.turn_hbm, ...), custom_call_target="tpu_custom_call" | custom-call | flops 268435456 | bytes 3674112 | tf_op jit(solution)/shard_map/forward_y/pallas_call | solution.py:108
  45.6 12.8 %all_to_all.25.got_ref = f32[4,256,128]{2,1,0:T(8,128)S(1)} all-to-all(f32[4,256,128]{2,1,0:T(8,128)S(1)} %get-tuple-element.36), channel_id=1, replica_groups=mesh['y'=4,'zl'=8,'c'=2,'zh'=2,'x'=4] {'x'}, dimensions={0} | all-to-all | bytes 1048576 | tf_op jit(solution)/shard_map/all_to_all | solution.py:723
  58.4 2.8 %solve_back.1 = (f32[384,128]{1,0:T(8,128)S(1)}, f32[3,1,16,1024]{3,2,1,0:T(8,128)S(1)}, s32[1,16,1024]{2,1,0:T(8,128)S(1)}, bf16[608,2048]{1,0:T(8,128)(2,1)S(1)}, bf16[288,640]{1,0:T(8,128)(2,1)S(1)}) custom-call(f32[4,256,128]{2,1,0:T(8,128)S(1)} %all_to_all.25.got_ref, f32[640,128]{1,0:T(8,128)S(1)} %get-tuple-element.37.turn_ref, ...), custom_call_target="tpu_custom_call" | custom-call | flops 268435456 | bytes 4497408 | tf_op jit(solution)/shard_map/solve_back/pallas_call | solution.py:108
  61.1 26.7 %all_to_all.26 = f32[128,1,384]{2,1,0:T(1,128)S(1)} all-to-all(f32[128,1,384]{2,1,0:T(1,128)S(1)} %bitcast.20), channel_id=1, replica_groups=mesh['y'=4,'zl'=8,'c'=2,'zh'=2,'x'=4] {'zh','y','zl','c'}, dimensions={0} | all-to-all | bytes 393216 | tf_op jit(solution)/shard_map/all_to_all | solution.py:632
  87.8 6.5 %closure_back.1 = (f32[352,128]{1,0:T(8,128)S(1)}, f32[3,1,16,1024]{3,2,1,0:T(8,128)}, f32[1,16,1024]{2,1,0:T(8,128)}) custom-call(f32[384,128]{1,0:T(8,128)S(1)} %bitcast.19, f32[640,128]{1,0:T(8,128)S(1)} %get-tuple-element.37.turn_ref, bf16[512,2048]{1,0:T(8,128)(2,1)S(1)} %get-tuple-element.41.second_ref, ...), custom_call_target="tpu_custom_call" | custom-call | flops 2952790016 | bytes 6266880 | tf_op jit(solution)/shard_map/closure_back/pallas_call | solution.py:108
  94.4 11.1 %all_to_all.27 = f32[32,1,1408]{2,1,0:T(1,128)S(1)} all-to-all(f32[32,1,1408]{2,1,0:T(1,128)S(1)} %bitcast.21), channel_id=1, replica_groups=mesh['y'=4,'zl'=8,'c'=2,'zh'=2,'x'=4] {'y','x','c'}, dimensions={0} | all-to-all | bytes 360448 | tf_op jit(solution)/shard_map/all_to_all | solution.py:632
  105.5 18.0 %all_to_all.28 = f32[16,1,1408]{2,1,0:T(1,128)S(1)} all-to-all(f32[16,1,1408]{2,1,0:T(1,128)S(1)} %bitcast.18), channel_id=1, replica_groups=mesh['y'=4,'zl'=8,'c'=2,'zh'=2,'x'=4] {'zl','zh'}, dimensions={0} | all-to-all | bytes 180224 | tf_op jit(solution)/shard_map/all_to_all | solution.py:632
  123.5 0.7 sum_column.1
  (1 shorter events, 0.0 us)
Async XLA Ops:
  3.6 39.8 %all-to-all-start = ((f32[128,1,384]{2,1,0:T(1,128)}), f32[128,1,384]{2,1,0:T(1,128)S(1)}, u32[]{:S(2)}, u32[]{:S(2)}) async-start(f32[128,1,384]{2,1,0:T(1,128)} %bitcast), calls=%async_computation | async-start | bytes 393216 | tf_op jit(solution)/shard_map/all_to_all | solution.py:632

commit v3 on v2

--- a/solution.py
+++ b/solution.py
@@ -70,9 +70,9 @@
     return jnp.dot(a, b, preferred_element_type=f32)
 
 
-def dot_table(table_ref, b):
-    rows = table_ref.shape[0] // 2
-    return dot(table_ref[0:rows], b) + dot(table_ref[rows : 2 * rows], b)
+def dot_table(table_ref, b, start, rows):
+    middle = start + rows
+    return dot(table_ref[start:middle], b) + dot(table_ref[middle : middle + rows], b)
 
 
 def dot_nt(a, b):
@@ -179,7 +179,7 @@
     )
     for copy in copies:
         copy.wait()
-    got = dot_table(table_ref, lines)
+    got = dot_table(table_ref, lines, 0, 512)
     cos_r, sin_r = [], []
     for r in range(4):
         cos_part = got[0:256, LANES * r : LANES * (r + 1)]
@@ -204,15 +204,15 @@
     return tuple(jnp.where(within < 8, a, b) for a, b in zip(one, two))
 
 
-def forward_y(msg_ref, table_hbm, turn_hbm, second_hbm, back_hbm, mark_ref,
-              out_ref, turn_ref, second_ref, back_ref, table_ref, sems):
+def forward_y(msg_ref, table_hbm, turn_hbm, back_hbm, wide_hbm, mark_ref,
+              out_ref, turn_ref, back_ref, wide_ref, table_ref, sems):
     copies = [
         start_copy(table_hbm, table_ref, sems, 0),
         start_copy(turn_hbm, turn_ref, sems, 1),
     ]
     later_copies = [
         start_copy(back_hbm, back_ref, sems, 2),
-        start_copy(second_hbm, second_ref, sems, 3),
+        start_copy(wide_hbm, wide_ref, sems, 3),
     ]
     within = lane_of((64, LANES)) % 16
     highs = []
@@ -246,7 +246,7 @@
     lines = jnp.concatenate(lines, axis=1)
     for copy in copies:
         copy.wait()
-    got = dot_table(table_ref, lines)
+    got = dot_table(table_ref, lines, 0, 512)
     within = lane_of((256, LANES)) % 16
     turned = [
         turn(
@@ -284,31 +284,32 @@
     return inv_dz, face, sub, base, sup, keep
 
 
-def solve_back(got_ref, turn_ref, table_hbm, cot_hbm, mask_hbm, first_hbm, wide_hbm,
-               out_ref, cot_ref, mask_ref, first_ref, wide_ref, table_ref, sems):
-    copies = [start_copy(table_hbm, table_ref, sems, 0)]
-    later_copies = [
-        start_copy(cot_hbm, cot_ref, sems, 1),
-        start_copy(mask_hbm, mask_ref, sems, 2),
-        start_copy(wide_hbm, wide_ref, sems, 3),
-        start_copy(first_hbm, first_ref, sems, 4),
-    ]
+def solve_back(got_ref, turn_ref, table_ref, out_ref):
     at = lax.axis_index("x")
     rows = got_ref.shape[1]
-    lam = turn_ref[256 : 256 + rows]
+    lam = turn_ref[256 : 256 + rows // 4]
     lane = lane_of((rows, LANES))
+    column = lane_of(lam.shape) % 4
     inv_dz, face, sub, base, sup, keep = (
         [turn_ref[512 + 8 * i + k : 513 + 8 * i + k] for k in range(LEVELS)]
         for i in range(6)
     )
+    quarters = [slice(rows // 4 * r, rows // 4 * (r + 1)) for r in range(4)]
+
+    def gathered(k, field):
+        at_lane = 2 * (k // 4) + field
+        value = roll(got_ref[k % 4, quarters[0], :], -at_lane, 1)
+        for r in range(1, 4):
+            moved = roll(got_ref[k % 4, quarters[r], :], r - at_lane, 1)
+            value = jnp.where(column == r, moved, value)
+        return value
+
     ratios = []
     values = []
     below = None
     for k in range(LEVELS):
-        packed = got_ref[k % 4]
-        half = k // 4
-        flux = roll(packed, -(2 * half + 1), 1) * face[k]
-        right = roll(packed, -2 * half, 1) - flux
+        flux = gathered(k, 1) * face[k]
+        right = gathered(k, 0) - flux
         if k > 0:
             right = right + below
         below = flux
@@ -332,13 +333,14 @@
             value = jnp.where(at == x, items[4 * half + x], value)
         return value
 
-    column = lane % 4
-    both = own(result, 0)
-    both = jnp.where(column == 1, roll(own(change, 0), 1, 1), both)
-    both = jnp.where(column == 2, roll(own(result, 1), 2, 1), both)
-    both = jnp.where(column == 3, roll(own(change, 1), 3, 1), both)
-    for copy in copies:
-        copy.wait()
+    fields = [own(result, 0), own(change, 0), own(result, 1), own(change, 1)]
+    both = []
+    for r in range(4):
+        value = roll(fields[0], -r, 1)
+        for c in range(1, 4):
+            value = jnp.where(column == c, roll(fields[c], c - r, 1), value)
+        both.append(value)
+    both = jnp.concatenate(both, axis=0)
     within = lane % 16
     blocks = []
     for g in range(4):
@@ -354,7 +356,7 @@
             high, low = split_f32(jnp.where(within % 8 < 4, value, 0.0))
             parts[i].append((high + roll(low, 4, 1)).astype(bf16))
     columns = jnp.concatenate([jnp.concatenate(part, axis=1) for part in parts], axis=0)
-    got = dot_table(table_ref, columns)
+    got = dot_table(table_ref, columns, 512, 256)
     within = lane_of((64, LANES)) % 16
     packed = [jnp.zeros((64, LANES), f32)] * 4
     for pair in range(2):
@@ -374,8 +376,6 @@
         )
         for field, value in enumerate((pressure, change_up, before - pressure)):
             out_ref[pl.ds(192 * half + field, 64, stride=3), :] = value
-    for copy in later_copies:
-        copy.wait()
 
 
 CHUNK = 1024
@@ -508,7 +508,7 @@
             high, low = split_f32(value)
             parts[i].append((high + roll(low, 64, 1)).astype(bf16))
     columns = jnp.concatenate([jnp.concatenate(part, axis=1) for part in parts], axis=0)
-    found = dot_table(table_ref, columns)
+    found = dot_table(table_ref, columns, 0, 256)
     for r in range(4):
         block = found[:, LANES * r : LANES * (r + 1)]
         line_ref[pl.ds(r, 256, stride=4), :] = block + roll(block, 64, 1)
@@ -639,12 +639,12 @@
     span_y = rows * 64
     table = dft_table(256, 1024)
     table_y = table[:, (np.arange(256) % 64) * 4 + np.arange(256) // 64]
-    x_table, y_table, x_back, y_back = (
-        jnp.asarray(two_parts(item)) for item in (table, table_y, table.T, table_y.T)
-    )
+    x_table, y_table = jnp.asarray(two_parts(table)), jnp.asarray(two_parts(table_y))
+    backs = jnp.asarray(np.concatenate([two_parts(table.T), two_parts(table_y.T)], axis=0))
     eigen = eigenvalue(width)
     lanes = np.arange(LANES)
-    ey = eigen.reshape(4, 256)[lanes % 16 // 4].T.astype(np.float32)
+    ey = eigen.reshape(4, 4, 64)[lanes % 16 // 4, lanes % 4].T.astype(np.float32)
+    ey = np.concatenate([ey, np.zeros((192, LANES), np.float32)], axis=0)
     ex = eigen[np.arange(128)[:, None] + 128 * (lanes[None, :] // 16)].astype(np.float32)
     turns = twiddles(256, 1024)
     fixed = jnp.asarray(np.concatenate([turns, ey, ex], axis=0))
@@ -653,7 +653,7 @@
     dma = pltpu.SemaphoreType.DMA
     type_of = jax.ShapeDtypeStruct
     table = pltpu.VMEM((1024, 256), bf16)
-    back_table = pltpu.VMEM((512, 512), bf16)
+    back_tables = pltpu.VMEM((1024, 512), bf16)
     turn_held = pltpu.VMEM((640, LANES), f32)
     first_held = pltpu.VMEM((608, cells), bf16)
     second_held = pltpu.VMEM((512, cells), bf16)
@@ -711,28 +711,20 @@
         flops=2 * 256 * 256 * cells * 4,
         name="closure_forward",
     )
-    gathered, turns, second, x_back = call(
+    gathered, turns, backs, weights = call(
         forward_y,
-        (type_of((4, 256, LANES), f32), turn_held, second_held, back_table),
-        (msg, y_table, turns, second, x_back, mark),
-        hbm=range(1, 5),
+        (type_of((4, 256, LANES), f32), turn_held, back_tables, wide_held),
+        (msg, y_table, turns, backs, weights, mark),
+        hbm=(1, 2, 3, 4),
         scratch=(table, dma((4,))),
         flops=table_flops,
         name="forward_y",
     )
     gathered = lax.all_to_all(gathered, "x", 0, 0)
-    msg, cotangent, cell_mask, first, weights = call(
+    (msg,) = call(
         solve_back,
-        (
-            msg_type,
-            pltpu.VMEM(cotangent.shape, f32),
-            pltpu.VMEM(cell_mask.shape, jnp.int32),
-            first_held,
-            wide_held,
-        ),
-        (gathered, turns, y_back, cotangent, cell_mask, first, weights),
-        hbm=range(2, 7),
-        scratch=(back_table, dma((5,))),
+        (msg_type,),
+        (gathered, turns, backs),
         flops=table_flops,
         name="solve_back",
     )
@@ -744,7 +736,7 @@
             pltpu.HBM(cotangent.shape, f32),
             pltpu.HBM(buoyancy.shape, f32),
         ),
-        (msg, turns, second, x_back, cotangent, cell_mask, first, weights),
+        (msg, turns, second, backs, cotangent, cell_mask, first, weights),
         hbm_out=(1, 2),
         scratch=(
             pltpu.VMEM((1024, LANES), f32),

time: 125 us -> 124 us (level)
  no operation moved by 1% of the time
where the time goes in v3:
time: 124 us
  blocking collectives  68.5 us (55%)
  Pallas kernels  19.3 us (16%)
  starting transfers between devices  19.2 us (15%)
  waiting for transfers between devices  16.1 us (13%)
    all_to_all x3, blocking collectives, trade(): got = lax.all_to_all(rows.reshape(peers, 1, size), axes, 0, 0)  55.8 us
    pallas_call x7, Pallas kernels, call(): pl.pallas_call(kernel, out_shape=out_shape, in_specs=[space(i, held) for...  19.3 us
    all_to_all x1, starting transfers between devices, trade(): got = lax.all_to_all(rows.reshape(peers, 1, size), axes, 0, 0)  19.2 us
    all_to_all x1, waiting for transfers between devices, trade(): got = lax.all_to_all(rows.reshape(peers, 1, size), axes, 0, 0)  16.1 us
    all_to_all x1, blocking collectives, shards(): gathered = lax.all_to_all(gathered, 'x', 0, 0)  12.8 us
  transfers between devices with their start and end apart: 1, of which 1 were waited for; matrix products, arithmetic and copies ran while one was open for 0% of the time, Pallas kernels for 4%

profile of v3, /device:TPU:32, one launch (start us, length us, event | category | flops | bytes accessed | tf_op | source)
XLA Modules:
  0.0 123.7 jit_solution(13622414905499336943)
XLA Ops:
  0.6 3.0 %forward_x.1 = (f32[384,128]{1,0:T(8,128)}, f32[8,128]{1,0:T(8,128)S(1)}) custom-call(f32[3,1,16,1024]{3,2,1,0:T(8,128)} %cot_ref.1, bf16[1024,256]{1,0:T(8,128)(2,1)} %constant.10.clone.table_hbm, f32[256,128]{1,0:T(8,128)} %constant.14.clone.turn_hbm), custom_call_target="tpu_custom_call" | custom-call | flops 268435456 | bytes 851968 | tf_op jit(solution)/shard_map/forward_x/pallas_call | solution.py:108
  3.6 19.2 %all-to-all-start = ((f32[128,1,384]{2,1,0:T(1,128)}), f32[128,1,384]{2,1,0:T(1,128)S(1)}, u32[]{:S(2)}, u32[]{:S(2)}) async-start(f32[128,1,384]{2,1,0:T(1,128)} %bitcast), calls=%async_computation | async-start | bytes 393216 | tf_op jit(solution)/shard_map/all_to_all | solution.py:632
  22.8 4.6 %closure_forward.1 = (bf16[608,2048]{1,0:T(8,128)(2,1)}, bf16[512,2048]{1,0:T(8,128)(2,1)}, bf16[288,640]{1,0:T(8,128)(2,1)}, f32[640,128]{1,0:T(8,128)}, f32[8,128]{1,0:T(8,128)S(1)}) custom-call(f32[4,32]{1,0:T(4,128)} %bitcast.22, f32[1,32]{1,0:T(1,128)} %bitcast.24, f32[32,32]{1,0:T(8,128)} %wmid_hbm.1, f32[1,32]{1,0:T(1,128)} %bitcast.25, ...), custom_call_target="tpu_custom_call" | custom-call | flops 1073741824 | bytes 599200 | tf_op jit(solution)/shard_map/closure_forward/pallas_call | solution.py:108
  27.4 16.1 %all-to-all-done = f32[128,1,384]{2,1,0:T(1,128)S(1)} async-done(((f32[128,1,384]{2,1,0:T(1,128)}), f32[128,1,384]{2,1,0:T(1,128)S(1)}, u32[]{:S(2)}, u32[]{:S(2)}) %all-to-all-start) | async-done | bytes 196640 | tf_op jit(solution)/shard_map/all_to_all | solution.py:632
  43.5 0.0 copy-start
  43.5 0.0 copy-start.1
  43.5 0.0 copy-start.2
  43.5 0.0 copy-start.3
  43.5 2.2 %forward_y.1 = (f32[4,256,128]{2,1,0:T(8,128)S(1)}, f32[640,128]{1,0:T(8,128)S(1)}, bf16[1024,512]{1,0:T(8,128)(2,1)S(1)}, bf16[288,640]{1,0:T(8,128)(2,1)S(1)}) custom-call(f32[384,128]{1,0:T(8,128)S(1)} %bitcast.15, bf16[1024,256]{1,0:T(8,128)(2,1)} %constant.11.clone.table_hbm, f32[640,128]{1,0:T(8,128)} %get-tuple-element.28.turn_hbm, ...), custom_call_target="tpu_custom_call" | custom-call | flops 268435456 | bytes 2469888 | tf_op jit(solution)/shard_map/forward_y/pallas_call | solution.py:108
  45.7 12.8 %all_to_all.25.got_ref = f32[4,256,128]{2,1,0:T(8,128)S(1)} all-to-all(f32[4,256,128]{2,1,0:T(8,128)S(1)} %get-tuple-element.31), channel_id=1, replica_groups=mesh['y'=4,'zl'=8,'c'=2,'zh'=2,'x'=4] {'x'}, dimensions={0} | all-to-all | bytes 1048576 | tf_op jit(solution)/shard_map/all_to_all | solution.py:723
  58.4 2.3 %solve_back.1 = f32[384,128]{1,0:T(8,128)S(1)} custom-call(f32[4,256,128]{2,1,0:T(8,128)S(1)} %all_to_all.25.got_ref, f32[640,128]{1,0:T(8,128)S(1)} %get-tuple-element.32.turn_ref, bf16[1024,512]{1,0:T(8,128)(2,1)S(1)} %get-tuple-element.33.table_ref), custom_call_target="tpu_custom_call" | custom-call | flops 268435456 | bytes 1900544 | tf_op jit(solution)/shard_map/solve_back/pallas_call | solution.py:108
  60.8 26.7 %all_to_all.26 = f32[128,1,384]{2,1,0:T(1,128)S(1)} all-to-all(f32[128,1,384]{2,1,0:T(1,128)S(1)} %bitcast.16), channel_id=1, replica_groups=mesh['y'=4,'zl'=8,'c'=2,'zh'=2,'x'=4] {'zh','y','zl','c'}, dimensions={0} | all-to-all | bytes 393216 | tf_op jit(solution)/shard_map/all_to_all | solution.py:632
  87.5 0.0 copy-done
  87.5 0.0 copy-done.1
  87.5 0.0 copy-done.2
  87.5 0.0 copy-done.3
  87.5 6.5 %closure_back.1 = (f32[352,128]{1,0:T(8,128)S(1)}, f32[3,1,16,1024]{3,2,1,0:T(8,128)}, f32[1,16,1024]{2,1,0:T(8,128)}) custom-call(f32[384,128]{1,0:T(8,128)S(1)} %bitcast.20, f32[640,128]{1,0:T(8,128)S(1)} %get-tuple-element.32.turn_ref, bf16[512,2048]{1,0:T(8,128)(2,1)S(1)} %copy-done.3, bf16[1024,512]{1,0:T(8,128)(2,1)S(1)} %get-tuple-element.33.table_ref, ...), custom_call_target="tpu_custom_call" | custom-call | flops 2952790016 | bytes 6791168 | tf_op jit(solution)/shard_map/closure_back/pallas_call | solution.py:108
  94.0 11.1 %all_to_all.27 = f32[32,1,1408]{2,1,0:T(1,128)S(1)} all-to-all(f32[32,1,1408]{2,1,0:T(1,128)S(1)} %bitcast.21), channel_id=1, replica_groups=mesh['y'=4,'zl'=8,'c'=2,'zh'=2,'x'=4] {'y','x','c'}, dimensions={0} | all-to-all | bytes 360448 | tf_op jit(solution)/shard_map/all_to_all | solution.py:632
  105.1 18.0 %all_to_all.28 = f32[16,1,1408]{2,1,0:T(1,128)S(1)} all-to-all(f32[16,1,1408]{2,1,0:T(1,128)S(1)} %bitcast.19), channel_id=1, replica_groups=mesh['y'=4,'zl'=8,'c'=2,'zh'=2,'x'=4] {'zl','zh'}, dimensions={0} | all-to-all | bytes 180224 | tf_op jit(solution)/shard_map/all_to_all | solution.py:632
  123.0 0.7 sum_column.1
  (1 shorter events, 0.0 us)
Async XLA Ops:
  3.6 39.8 %all-to-all-start = ((f32[128,1,384]{2,1,0:T(1,128)}), f32[128,1,384]{2,1,0:T(1,128)S(1)}, u32[]{:S(2)}, u32[]{:S(2)}) async-start(f32[128,1,384]{2,1,0:T(1,128)} %bitcast), calls=%async_computation | async-start | bytes 393216 | tf_op jit(solution)/shard_map/all_to_all | solution.py:632
  43.5 44.0 %copy-start = (f32[3,1,16,1024]{3,2,1,0:T(8,128)S(1)}, f32[3,1,16,1024]{3,2,1,0:T(8,128)}, u32[]{:S(2)}) copy-start(f32[3,1,16,1024]{3,2,1,0:T(8,128)} %cot_ref.1) | copy-start | bytes 589828
  43.5 44.0 %copy-start.1 = (s32[1,16,1024]{2,1,0:T(8,128)S(1)}, s32[1,16,1024]{2,1,0:T(8,128)}, u32[]{:S(2)}) copy-start(s32[1,16,1024]{2,1,0:T(8,128)} %mask_ref.1) | copy-start | bytes 196612
  43.5 44.0 %copy-start.2 = (bf16[608,2048]{1,0:T(8,128)(2,1)S(1)}, bf16[608,2048]{1,0:T(8,128)(2,1)}, u32[]{:S(2)}) copy-start(bf16[608,2048]{1,0:T(8,128)(2,1)} %get-tuple-element.35.first_ref) | copy-start | bytes 7471108
  43.5 44.0 %copy-start.3 = (bf16[512,2048]{1,0:T(8,128)(2,1)S(1)}, bf16[512,2048]{1,0:T(8,128)(2,1)}, u32[]{:S(2)}) copy-start(bf16[512,2048]{1,0:T(8,128)(2,1)} %get-tuple-element.34.second_ref) | copy-start | bytes 6291460

commit v4 on v3

--- a/solution.py
+++ b/solution.py
@@ -21,9 +21,9 @@
 FINE = (("y", 4), ("zl", 8), ("c", 2), ("zh", 2), ("x", 4))
 WIDE = ("y", "zl", "c")
 NARROW = ("zh", "x")
-PLANE = ("zh", "y", "zl", "c")
+PLANE = ("y", "zl", "c", "zh")
 SLAB = ("y", "x", "c")
-COLUMN = ("zl", "zh")
+COLUMN = ("zh", "zl")
 
 
 def dft_table(count, length):
@@ -219,7 +219,7 @@
     lows = []
     for half in range(2):
         east, north, up = (
-            msg_ref[pl.ds(192 * half + field, 64, stride=3), :] for field in range(3)
+            msg_ref[pl.ds(3 * half + field, 64, stride=6), :] for field in range(3)
         )
         after = jnp.where(
             within < 15, roll(north, -1, 1), roll(roll(north, -1, 0), 15, 1)
@@ -375,7 +375,7 @@
             within > 0, roll(pressure, 1, 1), roll(roll(pressure, 1, 0), -15, 1)
         )
         for field, value in enumerate((pressure, change_up, before - pressure)):
-            out_ref[pl.ds(192 * half + field, 64, stride=3), :] = value
+            out_ref[pl.ds(3 * half + field, 64, stride=6), :] = value
 
 
 CHUNK = 1024

time: 124 us -> 124 us (level)
  no operation moved by 1% of the time
where the time goes in v4:
time: 124 us; the launch traced here: 123 us
  blocking collectives  68 us (55%)
  Pallas kernels  19.3 us (16%)
  starting transfers between devices  19.2 us (15%)
  waiting for transfers between devices  16 us (13%)
    all_to_all x3, blocking collectives, trade(): got = lax.all_to_all(rows.reshape(peers, 1, size), axes, 0, 0)  54.7 us
    pallas_call x7, Pallas kernels, call(): pl.pallas_call(kernel, out_shape=out_shape, in_specs=[space(i, held) for...  19.3 us
    all_to_all x1, starting transfers between devices, trade(): got = lax.all_to_all(rows.reshape(peers, 1, size), axes, 0, 0)  19.2 us
    all_to_all x1, waiting for transfers between devices, trade(): got = lax.all_to_all(rows.reshape(peers, 1, size), axes, 0, 0)  16 us
    all_to_all x1, blocking collectives, shards(): gathered = lax.all_to_all(gathered, 'x', 0, 0)  13.3 us
  transfers between devices with their start and end apart: 1, of which 1 were waited for; matrix products, arithmetic and copies ran while one was open for 0% of the time, Pallas kernels for 4%

profile of v4, /device:TPU:32, one launch (start us, length us, event | category | flops | bytes accessed | tf_op | source)
XLA Modules:
  0.0 123.2 jit_solution(17019462907961684789)
XLA Ops:
  0.6 3.0 %forward_x.1 = (f32[384,128]{1,0:T(8,128)}, f32[8,128]{1,0:T(8,128)S(1)}) custom-call(f32[3,1,16,1024]{3,2,1,0:T(8,128)} %cot_ref.1, bf16[1024,256]{1,0:T(8,128)(2,1)} %constant.10.clone.table_hbm, f32[256,128]{1,0:T(8,128)} %constant.14.clone.turn_hbm), custom_call_target="tpu_custom_call" | custom-call | flops 268435456 | bytes 851968 | tf_op jit(solution)/shard_map/forward_x/pallas_call | solution.py:108
  3.6 19.2 %all-to-all-start = ((f32[128,1,384]{2,1,0:T(1,128)}), f32[128,1,384]{2,1,0:T(1,128)S(1)}, u32[]{:S(2)}, u32[]{:S(2)}) async-start(f32[128,1,384]{2,1,0:T(1,128)} %bitcast), calls=%async_computation | async-start | bytes 393216 | tf_op jit(solution)/shard_map/all_to_all | solution.py:632
  22.8 4.6 %closure_forward.1 = (bf16[608,2048]{1,0:T(8,128)(2,1)}, bf16[512,2048]{1,0:T(8,128)(2,1)}, bf16[288,640]{1,0:T(8,128)(2,1)}, f32[640,128]{1,0:T(8,128)}, f32[8,128]{1,0:T(8,128)S(1)}) custom-call(f32[4,32]{1,0:T(4,128)} %bitcast.22, f32[1,32]{1,0:T(1,128)} %bitcast.24, f32[32,32]{1,0:T(8,128)} %wmid_hbm.1, f32[1,32]{1,0:T(1,128)} %bitcast.25, ...), custom_call_target="tpu_custom_call" | custom-call | flops 1073741824 | bytes 599200 | tf_op jit(solution)/shard_map/closure_forward/pallas_call | solution.py:108
  27.4 16.0 %all-to-all-done = f32[128,1,384]{2,1,0:T(1,128)S(1)} async-done(((f32[128,1,384]{2,1,0:T(1,128)}), f32[128,1,384]{2,1,0:T(1,128)S(1)}, u32[]{:S(2)}, u32[]{:S(2)}) %all-to-all-start) | async-done | bytes 196640 | tf_op jit(solution)/shard_map/all_to_all | solution.py:632
  43.4 0.0 copy-start
  43.4 0.0 copy-start.1
  43.4 0.0 copy-start.2
  43.4 0.0 copy-start.3
  43.5 2.2 %forward_y.1 = (f32[4,256,128]{2,1,0:T(8,128)S(1)}, f32[640,128]{1,0:T(8,128)S(1)}, bf16[1024,512]{1,0:T(8,128)(2,1)S(1)}, bf16[288,640]{1,0:T(8,128)(2,1)S(1)}) custom-call(f32[384,128]{1,0:T(8,128)S(1)} %bitcast.15, bf16[1024,256]{1,0:T(8,128)(2,1)} %constant.11.clone.table_hbm, f32[640,128]{1,0:T(8,128)} %get-tuple-element.28.turn_hbm, ...), custom_call_target="tpu_custom_call" | custom-call | flops 268435456 | bytes 2469888 | tf_op jit(solution)/shard_map/forward_y/pallas_call | solution.py:108
  45.7 13.3 %all_to_all.25.got_ref = f32[4,256,128]{2,1,0:T(8,128)S(1)} all-to-all(f32[4,256,128]{2,1,0:T(8,128)S(1)} %get-tuple-element.31), channel_id=1, replica_groups=mesh['y'=4,'zl'=8,'c'=2,'zh'=2,'x'=4] {'x'}, dimensions={0} | all-to-all | bytes 1048576 | tf_op jit(solution)/shard_map/all_to_all | solution.py:723
  59.0 2.3 %solve_back.1 = f32[384,128]{1,0:T(8,128)S(1)} custom-call(f32[4,256,128]{2,1,0:T(8,128)S(1)} %all_to_all.25.got_ref, f32[640,128]{1,0:T(8,128)S(1)} %get-tuple-element.32.turn_ref, bf16[1024,512]{1,0:T(8,128)(2,1)S(1)} %get-tuple-element.33.table_ref), custom_call_target="tpu_custom_call" | custom-call | flops 268435456 | bytes 1900544 | tf_op jit(solution)/shard_map/solve_back/pallas_call | solution.py:108
  61.3 26.5 %all_to_all.26 = f32[128,1,384]{2,1,0:T(1,128)S(1)} all-to-all(f32[128,1,384]{2,1,0:T(1,128)S(1)} %bitcast.16), channel_id=1, replica_groups=mesh['y'=4,'zl'=8,'c'=2,'zh'=2,'x'=4] {'y','zl','c','zh'}, dimensions={0} | all-to-all | bytes 393216 | tf_op jit(solution)/shard_map/all_to_all | solution.py:632
  87.8 0.0 copy-done
  87.8 0.0 copy-done.1
  87.8 0.0 copy-done.2
  87.8 0.0 copy-done.3
  87.8 6.5 %closure_back.1 = (f32[352,128]{1,0:T(8,128)S(1)}, f32[3,1,16,1024]{3,2,1,0:T(8,128)}, f32[1,16,1024]{2,1,0:T(8,128)}) custom-call(f32[384,128]{1,0:T(8,128)S(1)} %bitcast.20, f32[640,128]{1,0:T(8,128)S(1)} %get-tuple-element.32.turn_ref, bf16[512,2048]{1,0:T(8,128)(2,1)S(1)} %copy-done.3, bf16[1024,512]{1,0:T(8,128)(2,1)S(1)} %get-tuple-element.33.table_ref, ...), custom_call_target="tpu_custom_call" | custom-call | flops 2952790016 | bytes 6791168 | tf_op jit(solution)/shard_map/closure_back/pallas_call | solution.py:108
  94.3 11.1 %all_to_all.27 = f32[32,1,1408]{2,1,0:T(1,128)S(1)} all-to-all(f32[32,1,1408]{2,1,0:T(1,128)S(1)} %bitcast.21), channel_id=1, replica_groups=mesh['y'=4,'zl'=8,'c'=2,'zh'=2,'x'=4] {'y','x','c'}, dimensions={0} | all-to-all | bytes 360448 | tf_op jit(solution)/shard_map/all_to_all | solution.py:632
  105.4 17.2 %all_to_all.28 = f32[16,1,1408]{2,1,0:T(1,128)S(1)} all-to-all(f32[16,1,1408]{2,1,0:T(1,128)S(1)} %bitcast.19), channel_id=1, replica_groups=mesh['y'=4,'zl'=8,'c'=2,'zh'=2,'x'=4] {'zh','zl'}, dimensions={0} | all-to-all | bytes 180224 | tf_op jit(solution)/shard_map/all_to_all | solution.py:632
  122.5 0.7 sum_column.1
  (1 shorter events, 0.0 us)
Async XLA Ops:
  3.6 39.8 %all-to-all-start = ((f32[128,1,384]{2,1,0:T(1,128)}), f32[128,1,384]{2,1,0:T(1,128)S(1)}, u32[]{:S(2)}, u32[]{:S(2)}) async-start(f32[128,1,384]{2,1,0:T(1,128)} %bitcast), calls=%async_computation | async-start | bytes 393216 | tf_op jit(solution)/shard_map/all_to_all | solution.py:632
  43.4 44.3 %copy-start = (f32[3,1,16,1024]{3,2,1,0:T(8,128)S(1)}, f32[3,1,16,1024]{3,2,1,0:T(8,128)}, u32[]{:S(2)}) copy-start(f32[3,1,16,1024]{3,2,1,0:T(8,128)} %cot_ref.1) | copy-start | bytes 589828
  43.4 44.3 %copy-start.1 = (s32[1,16,1024]{2,1,0:T(8,128)S(1)}, s32[1,16,1024]{2,1,0:T(8,128)}, u32[]{:S(2)}) copy-start(s32[1,16,1024]{2,1,0:T(8,128)} %mask_ref.1) | copy-start | bytes 196612
  43.4 44.3 %copy-start.2 = (bf16[608,2048]{1,0:T(8,128)(2,1)S(1)}, bf16[608,2048]{1,0:T(8,128)(2,1)}, u32[]{:S(2)}) copy-start(bf16[608,2048]{1,0:T(8,128)(2,1)} %get-tuple-element.35.first_ref) | copy-start | bytes 7471108
  43.4 44.3 %copy-start.3 = (bf16[512,2048]{1,0:T(8,128)(2,1)S(1)}, bf16[512,2048]{1,0:T(8,128)(2,1)}, u32[]{:S(2)}) copy-start(bf16[512,2048]{1,0:T(8,128)(2,1)} %get-tuple-element.34.second_ref) | copy-start | bytes 6291460

commit v5 on v4

--- a/solution.py
+++ b/solution.py
@@ -502,7 +502,8 @@
     for r in range(4):
         pair = (cos_r[r], sin_r[r])
         if r > 0:
-            cos_turn, sin_turn = turn_of(turn_ref, r)
+            at = 512 * (r - 1)
+            cos_turn, sin_turn = turn_ref[at : at + 256], turn_ref[at + 256 : at + 512]
             pair = turn(*pair, cos_turn, -sin_turn)
         for i, value in enumerate(pair):
             high, low = split_f32(value)
@@ -648,6 +649,9 @@
     ex = eigen[np.arange(128)[:, None] + 128 * (lanes[None, :] // 16)].astype(np.float32)
     turns = twiddles(256, 1024)
     fixed = jnp.asarray(np.concatenate([turns, ey, ex], axis=0))
+    spread_turns = jnp.asarray(
+        np.concatenate([np.repeat(turns[:, i : i + 1], LANES, axis=1) for i in range(2, 8)], axis=0)
+    )
     turns = jnp.asarray(turns)
     cells = rows * width // 8
     dma = pltpu.SemaphoreType.DMA
@@ -736,7 +740,7 @@
             pltpu.HBM(cotangent.shape, f32),
             pltpu.HBM(buoyancy.shape, f32),
         ),
-        (msg, turns, second, backs, cotangent, cell_mask, first, weights),
+        (msg, spread_turns, second, backs, cotangent, cell_mask, first, weights),
         hbm_out=(1, 2),
         scratch=(
             pltpu.VMEM((1024, LANES), f32),

time: 124 us -> 123 us (level)
  no operation moved by 1% of the time
where the time goes in v5:
time: 123 us
  blocking collectives  68.2 us (55%)
  starting transfers between devices  19.2 us (16%)
  Pallas kernels  19 us (15%)
  waiting for transfers between devices  16 us (13%)
    all_to_all x3, blocking collectives, trade(): got = lax.all_to_all(rows.reshape(peers, 1, size), axes, 0, 0)  54.7 us
    all_to_all x1, starting transfers between devices, trade(): got = lax.all_to_all(rows.reshape(peers, 1, size), axes, 0, 0)  19.2 us
    pallas_call x7, Pallas kernels, call(): pl.pallas_call(kernel, out_shape=out_shape, in_specs=[space(i, held) for...  19 us
    all_to_all x1, waiting for transfers between devices, trade(): got = lax.all_to_all(rows.reshape(peers, 1, size), axes, 0, 0)  16 us
    all_to_all x1, blocking collectives, shards(): gathered = lax.all_to_all(gathered, 'x', 0, 0)  13.4 us
  transfers between devices with their start and end apart: 1, of which 1 were waited for; matrix products, arithmetic and copies ran while one was open for 0% of the time, Pallas kernels for 4%

profile of v5, /device:TPU:32, one launch (start us, length us, event | category | flops | bytes accessed | tf_op | source)
XLA Modules:
  0.0 123.0 jit_solution(7039044428201819406)
XLA Ops:
  0.6 3.0 %forward_x.1 = (f32[384,128]{1,0:T(8,128)}, f32[8,128]{1,0:T(8,128)S(1)}) custom-call(f32[3,1,16,1024]{3,2,1,0:T(8,128)} %cot_ref.1, bf16[1024,256]{1,0:T(8,128)(2,1)} %constant.12.clone.table_hbm, f32[256,128]{1,0:T(8,128)} %constant.17.clone.turn_hbm), custom_call_target="tpu_custom_call" | custom-call | flops 268435456 | bytes 851968 | tf_op jit(solution)/shard_map/forward_x/pallas_call | solution.py:108
  3.6 19.2 %all-to-all-start = ((f32[128,1,384]{2,1,0:T(1,128)}), f32[128,1,384]{2,1,0:T(1,128)S(1)}, u32[]{:S(2)}, u32[]{:S(2)}) async-start(f32[128,1,384]{2,1,0:T(1,128)} %bitcast), calls=%async_computation | async-start | bytes 393216 | tf_op jit(solution)/shard_map/all_to_all | solution.py:633
  22.8 4.6 %closure_forward.1 = (bf16[608,2048]{1,0:T(8,128)(2,1)}, bf16[512,2048]{1,0:T(8,128)(2,1)}, bf16[288,640]{1,0:T(8,128)(2,1)}, f32[640,128]{1,0:T(8,128)}, f32[8,128]{1,0:T(8,128)S(1)}) custom-call(f32[4,32]{1,0:T(4,128)} %bitcast.22, f32[1,32]{1,0:T(1,128)} %bitcast.24, f32[32,32]{1,0:T(8,128)} %wmid_hbm.1, f32[1,32]{1,0:T(1,128)} %bitcast.25, ...), custom_call_target="tpu_custom_call" | custom-call | flops 1073741824 | bytes 599200 | tf_op jit(solution)/shard_map/closure_forward/pallas_call | solution.py:108
  27.4 16.0 %all-to-all-done = f32[128,1,384]{2,1,0:T(1,128)S(1)} async-done(((f32[128,1,384]{2,1,0:T(1,128)}), f32[128,1,384]{2,1,0:T(1,128)S(1)}, u32[]{:S(2)}, u32[]{:S(2)}) %all-to-all-start) | async-done | bytes 196640 | tf_op jit(solution)/shard_map/all_to_all | solution.py:633
  43.4 0.0 copy-start
  43.4 0.0 copy-start.1
  43.4 0.0 copy-start.2
  43.4 0.0 copy-start.3
  43.5 0.0 copy-start.4
  43.5 2.2 %forward_y.1 = (f32[4,256,128]{2,1,0:T(8,128)S(1)}, f32[640,128]{1,0:T(8,128)S(1)}, bf16[1024,512]{1,0:T(8,128)(2,1)S(1)}, bf16[288,640]{1,0:T(8,128)(2,1)S(1)}) custom-call(f32[384,128]{1,0:T(8,128)S(1)} %bitcast.15, bf16[1024,256]{1,0:T(8,128)(2,1)} %constant.13.clone.table_hbm, f32[640,128]{1,0:T(8,128)} %get-tuple-element.28.turn_hbm, ...), custom_call_target="tpu_custom_call" | custom-call | flops 268435456 | bytes 2469888 | tf_op jit(solution)/shard_map/forward_y/pallas_call | solution.py:108
  45.7 13.4 %all_to_all.25.got_ref = f32[4,256,128]{2,1,0:T(8,128)S(1)} all-to-all(f32[4,256,128]{2,1,0:T(8,128)S(1)} %get-tuple-element.31), channel_id=1, replica_groups=mesh['y'=4,'zl'=8,'c'=2,'zh'=2,'x'=4] {'x'}, dimensions={0} | all-to-all | bytes 1048576 | tf_op jit(solution)/shard_map/all_to_all | solution.py:727
  59.1 2.3 %solve_back.1 = f32[384,128]{1,0:T(8,128)S(1)} custom-call(f32[4,256,128]{2,1,0:T(8,128)S(1)} %all_to_all.25.got_ref, f32[640,128]{1,0:T(8,128)S(1)} %get-tuple-element.32.turn_ref, bf16[1024,512]{1,0:T(8,128)(2,1)S(1)} %get-tuple-element.33.table_ref), custom_call_target="tpu_custom_call" | custom-call | flops 268435456 | bytes 1900544 | tf_op jit(solution)/shard_map/solve_back/pallas_call | solution.py:108
  61.4 26.5 %all_to_all.26 = f32[128,1,384]{2,1,0:T(1,128)S(1)} all-to-all(f32[128,1,384]{2,1,0:T(1,128)S(1)} %bitcast.16), channel_id=1, replica_groups=mesh['y'=4,'zl'=8,'c'=2,'zh'=2,'x'=4] {'y','zl','c','zh'}, dimensions={0} | all-to-all | bytes 393216 | tf_op jit(solution)/shard_map/all_to_all | solution.py:633
  87.9 0.0 copy-done
  87.9 0.0 copy-done.1
  87.9 0.0 copy-done.2
  87.9 0.0 copy-done.3
  87.9 0.0 copy-done.4
  87.9 6.1 %closure_back.1 = (f32[352,128]{1,0:T(8,128)S(1)}, f32[3,1,16,1024]{3,2,1,0:T(8,128)}, f32[1,16,1024]{2,1,0:T(8,128)}) custom-call(f32[384,128]{1,0:T(8,128)S(1)} %bitcast.20, f32[1536,128]{1,0:T(8,128)S(1)} %copy-done.2, bf16[512,2048]{1,0:T(8,128)(2,1)S(1)} %copy-done.4, bf16[1024,512]{1,0:T(8,128)(2,1)S(1)} %get-tuple-element.33.table_ref, ...), custom_call_target="tpu_custom_call" | custom-call | flops 2952790016 | bytes 7249920 | tf_op jit(solution)/shard_map/closure_back/pallas_call | solution.py:108
  94.1 11.1 %all_to_all.27 = f32[32,1,1408]{2,1,0:T(1,128)S(1)} all-to-all(f32[32,1,1408]{2,1,0:T(1,128)S(1)} %bitcast.21), channel_id=1, replica_groups=mesh['y'=4,'zl'=8,'c'=2,'zh'=2,'x'=4] {'y','x','c'}, dimensions={0} | all-to-all | bytes 360448 | tf_op jit(solution)/shard_map/all_to_all | solution.py:633
  105.2 17.2 %all_to_all.28 = f32[16,1,1408]{2,1,0:T(1,128)S(1)} all-to-all(f32[16,1,1408]{2,1,0:T(1,128)S(1)} %bitcast.19), channel_id=1, replica_groups=mesh['y'=4,'zl'=8,'c'=2,'zh'=2,'x'=4] {'zh','zl'}, dimensions={0} | all-to-all | bytes 180224 | tf_op jit(solution)/shard_map/all_to_all | solution.py:633
  122.3 0.7 sum_column.1
  (1 shorter events, 0.0 us)
Async XLA Ops:
  3.6 39.8 %all-to-all-start = ((f32[128,1,384]{2,1,0:T(1,128)}), f32[128,1,384]{2,1,0:T(1,128)S(1)}, u32[]{:S(2)}, u32[]{:S(2)}) async-start(f32[128,1,384]{2,1,0:T(1,128)} %bitcast), calls=%async_computation | async-start | bytes 393216 | tf_op jit(solution)/shard_map/all_to_all | solution.py:633
  43.4 44.5 %copy-start = (f32[3,1,16,1024]{3,2,1,0:T(8,128)S(1)}, f32[3,1,16,1024]{3,2,1,0:T(8,128)}, u32[]{:S(2)}) copy-start(f32[3,1,16,1024]{3,2,1,0:T(8,128)} %cot_ref.1) | copy-start | bytes 589828
  43.4 44.5 %copy-start.1 = (s32[1,16,1024]{2,1,0:T(8,128)S(1)}, s32[1,16,1024]{2,1,0:T(8,128)}, u32[]{:S(2)}) copy-start(s32[1,16,1024]{2,1,0:T(8,128)} %mask_ref.1) | copy-start | bytes 196612
  43.4 44.5 %copy-start.2 = (f32[1536,128]{1,0:T(8,128)S(1)}, f32[1536,128]{1,0:T(8,128)}, u32[]{:S(2)}) copy-start(f32[1536,128]{1,0:T(8,128)} %constant.16.clone.turn_ref) | copy-start | bytes 2359300
  43.4 44.5 %copy-start.3 = (bf16[608,2048]{1,0:T(8,128)(2,1)S(1)}, bf16[608,2048]{1,0:T(8,128)(2,1)}, u32[]{:S(2)}) copy-start(bf16[608,2048]{1,0:T(8,128)(2,1)} %get-tuple-element.35.first_ref) | copy-start | bytes 7471108
  43.5 44.5 %copy-start.4 = (bf16[512,2048]{1,0:T(8,128)(2,1)S(1)}, bf16[512,2048]{1,0:T(8,128)(2,1)}, u32[]{:S(2)}) copy-start(bf16[512,2048]{1,0:T(8,128)(2,1)} %get-tuple-element.34.second_ref) | copy-start | bytes 6291460

commit v6 on v5

--- a/solution.py
+++ b/solution.py
@@ -284,7 +284,7 @@
     return inv_dz, face, sub, base, sup, keep
 
 
-def solve_back(got_ref, turn_ref, table_ref, out_ref):
+def solve_back(got_ref, turn_ref, table_ref, pair_ref, out_ref):
     at = lax.axis_index("x")
     rows = got_ref.shape[1]
     lam = turn_ref[256 : 256 + rows // 4]
@@ -351,7 +351,8 @@
     for pair in range(2):
         cos_part = jnp.where(within < 8, cos_r[2 * pair], cos_r[2 * pair + 1])
         sin_part = jnp.where(within < 8, sin_r[2 * pair], sin_r[2 * pair + 1])
-        cos_turn, sin_turn = pair_turns(turn_ref, pair, within)
+        at = 512 * pair
+        cos_turn, sin_turn = pair_ref[at : at + 256], pair_ref[at + 256 : at + 512]
         for i, value in enumerate(turn(cos_part, sin_part, cos_turn, -sin_turn)):
             high, low = split_f32(jnp.where(within % 8 < 4, value, 0.0))
             parts[i].append((high + roll(low, 4, 1)).astype(bf16))
@@ -652,6 +653,12 @@
     spread_turns = jnp.asarray(
         np.concatenate([np.repeat(turns[:, i : i + 1], LANES, axis=1) for i in range(2, 8)], axis=0)
     )
+    pair_turns_held = jnp.asarray(
+        np.concatenate(
+            [turns[:, 4 * pair + i + 2 * (lanes % 16 // 8)] for pair in range(2) for i in range(2)],
+            axis=0,
+        )
+    )
     turns = jnp.asarray(turns)
     cells = rows * width // 8
     dma = pltpu.SemaphoreType.DMA
@@ -728,7 +735,7 @@
     (msg,) = call(
         solve_back,
         (msg_type,),
-        (gathered, turns, backs),
+        (gathered, turns, backs, pair_turns_held),
         flops=table_flops,
         name="solve_back",
     )

time: 123 us -> 123 us (level)
  no operation moved by 1% of the time
where the time goes in v6:
time: 123 us
  blocking collectives  68.3 us (56%)
  starting transfers between devices  19.2 us (16%)
  Pallas kernels  18.5 us (15%)
  waiting for transfers between devices  16 us (13%)
    all_to_all x3, blocking collectives, trade(): got = lax.all_to_all(rows.reshape(peers, 1, size), axes, 0, 0)  54.7 us
    all_to_all x1, starting transfers between devices, trade(): got = lax.all_to_all(rows.reshape(peers, 1, size), axes, 0, 0)  19.2 us
    pallas_call x7, Pallas kernels, call(): pl.pallas_call(kernel, out_shape=out_shape, in_specs=[space(i, held) for...  18.5 us
    all_to_all x1, waiting for transfers between devices, trade(): got = lax.all_to_all(rows.reshape(peers, 1, size), axes, 0, 0)  16 us
    all_to_all x1, blocking collectives, shards(): gathered = lax.all_to_all(gathered, 'x', 0, 0)  13.6 us
  transfers between devices with their start and end apart: 1, of which 1 were waited for; matrix products, arithmetic and copies ran while one was open for 0% of the time, Pallas kernels for 4%

profile of v6, /device:TPU:32, one launch (start us, length us, event | category | flops | bytes accessed | tf_op | source)
XLA Modules:
  0.0 122.7 jit_solution(3012406999427713798)
XLA Ops:
  0.6 3.0 %forward_x.1 = (f32[384,128]{1,0:T(8,128)}, f32[8,128]{1,0:T(8,128)S(1)}) custom-call(f32[3,1,16,1024]{3,2,1,0:T(8,128)} %cot_ref.1, bf16[1024,256]{1,0:T(8,128)(2,1)} %constant.14.clone.table_hbm, f32[256,128]{1,0:T(8,128)} %constant.20.clone.turn_hbm), custom_call_target="tpu_custom_call" | custom-call | flops 268435456 | bytes 851968 | tf_op jit(solution)/shard_map/forward_x/pallas_call | solution.py:108
  3.6 19.2 %all-to-all-start = ((f32[128,1,384]{2,1,0:T(1,128)}), f32[128,1,384]{2,1,0:T(1,128)S(1)}, u32[]{:S(2)}, u32[]{:S(2)}) async-start(f32[128,1,384]{2,1,0:T(1,128)} %bitcast), calls=%async_computation | async-start | bytes 393216 | tf_op jit(solution)/shard_map/all_to_all | solution.py:634
  22.8 4.6 %closure_forward.1 = (bf16[608,2048]{1,0:T(8,128)(2,1)}, bf16[512,2048]{1,0:T(8,128)(2,1)}, bf16[288,640]{1,0:T(8,128)(2,1)}, f32[640,128]{1,0:T(8,128)}, f32[8,128]{1,0:T(8,128)S(1)}) custom-call(f32[4,32]{1,0:T(4,128)} %bitcast.22, f32[1,32]{1,0:T(1,128)} %bitcast.24, f32[32,32]{1,0:T(8,128)} %wmid_hbm.1, f32[1,32]{1,0:T(1,128)} %bitcast.25, ...), custom_call_target="tpu_custom_call" | custom-call | flops 1073741824 | bytes 599200 | tf_op jit(solution)/shard_map/closure_forward/pallas_call | solution.py:108
  27.4 0.0 copy-start
  27.4 16.0 %all-to-all-done = f32[128,1,384]{2,1,0:T(1,128)S(1)} async-done(((f32[128,1,384]{2,1,0:T(1,128)}), f32[128,1,384]{2,1,0:T(1,128)S(1)}, u32[]{:S(2)}, u32[]{:S(2)}) %all-to-all-start) | async-done | bytes 196640 | tf_op jit(solution)/shard_map/all_to_all | solution.py:634
  43.4 0.0 copy-start.5
  43.4 2.2 %forward_y.1 = (f32[4,256,128]{2,1,0:T(8,128)S(1)}, f32[640,128]{1,0:T(8,128)S(1)}, bf16[1024,512]{1,0:T(8,128)(2,1)S(1)}, bf16[288,640]{1,0:T(8,128)(2,1)S(1)}) custom-call(f32[384,128]{1,0:T(8,128)S(1)} %bitcast.15, bf16[1024,256]{1,0:T(8,128)(2,1)} %constant.15.clone.table_hbm, f32[640,128]{1,0:T(8,128)} %get-tuple-element.28.turn_hbm, ...), custom_call_target="tpu_custom_call" | custom-call | flops 268435456 | bytes 2469888 | tf_op jit(solution)/shard_map/forward_y/pallas_call | solution.py:108
  45.6 0.0 copy-start.1
  45.7 0.0 copy-start.2
  45.7 0.0 copy-start.3
  45.7 0.0 copy-start.4
  45.7 13.6 %all_to_all.25.got_ref = f32[4,256,128]{2,1,0:T(8,128)S(1)} all-to-all(f32[4,256,128]{2,1,0:T(8,128)S(1)} %get-tuple-element.31), channel_id=1, replica_groups=mesh['y'=4,'zl'=8,'c'=2,'zh'=2,'x'=4] {'x'}, dimensions={0} | all-to-all | bytes 1048576 | tf_op jit(solution)/shard_map/all_to_all | solution.py:734
  59.3 0.0 copy-done
  59.3 1.8 %solve_back.1 = f32[384,128]{1,0:T(8,128)S(1)} custom-call(f32[4,256,128]{2,1,0:T(8,128)S(1)} %all_to_all.25.got_ref, f32[640,128]{1,0:T(8,128)S(1)} %get-tuple-element.32.turn_ref, bf16[1024,512]{1,0:T(8,128)(2,1)S(1)} %get-tuple-element.33.table_ref, f32[1024,128]{1,0:T(8,128)S(1)} %copy-done), custom_call_target="tpu_custom_call" | custom-call | flops 268435456 | bytes 2424832 | tf_op jit(solution)/shard_map/solve_back/pallas_call | solution.py:108
  61.1 26.5 %all_to_all.26 = f32[128,1,384]{2,1,0:T(1,128)S(1)} all-to-all(f32[128,1,384]{2,1,0:T(1,128)S(1)} %bitcast.16), channel_id=1, replica_groups=mesh['y'=4,'zl'=8,'c'=2,'zh'=2,'x'=4] {'y','zl','c','zh'}, dimensions={0} | all-to-all | bytes 393216 | tf_op jit(solution)/shard_map/all_to_all | solution.py:634
  87.6 0.0 copy-done.5
  87.6 0.0 copy-done.1
  87.6 0.0 copy-done.2
  87.6 0.0 copy-done.3
  87.6 0.0 copy-done.4
  87.6 6.1 %closure_back.1 = (f32[352,128]{1,0:T(8,128)S(1)}, f32[3,1,16,1024]{3,2,1,0:T(8,128)}, f32[1,16,1024]{2,1,0:T(8,128)}) custom-call(f32[384,128]{1,0:T(8,128)S(1)} %bitcast.20, f32[1536,128]{1,0:T(8,128)S(1)} %copy-done.3, bf16[512,2048]{1,0:T(8,128)(2,1)S(1)} %copy-done.5, bf16[1024,512]{1,0:T(8,128)(2,1)S(1)} %get-tuple-element.33.table_ref, ...), custom_call_target="tpu_custom_call" | custom-call | flops 2952790016 | bytes 7249920 | tf_op jit(solution)/shard_map/closure_back/pallas_call | solution.py:108
  93.8 11.1 %all_to_all.27 = f32[32,1,1408]{2,1,0:T(1,128)S(1)} all-to-all(f32[32,1,1408]{2,1,0:T(1,128)S(1)} %bitcast.21), channel_id=1, replica_groups=mesh['y'=4,'zl'=8,'c'=2,'zh'=2,'x'=4] {'y','x','c'}, dimensions={0} | all-to-all | bytes 360448 | tf_op jit(solution)/shard_map/all_to_all | solution.py:634
  104.9 17.2 %all_to_all.28 = f32[16,1,1408]{2,1,0:T(1,128)S(1)} all-to-all(f32[16,1,1408]{2,1,0:T(1,128)S(1)} %bitcast.19), channel_id=1, replica_groups=mesh['y'=4,'zl'=8,'c'=2,'zh'=2,'x'=4] {'zh','zl'}, dimensions={0} | all-to-all | bytes 180224 | tf_op jit(solution)/shard_map/all_to_all | solution.py:634
  122.0 0.7 sum_column.1
  (1 shorter events, 0.0 us)
Async XLA Ops:
  3.6 39.8 %all-to-all-start = ((f32[128,1,384]{2,1,0:T(1,128)}), f32[128,1,384]{2,1,0:T(1,128)S(1)}, u32[]{:S(2)}, u32[]{:S(2)}) async-start(f32[128,1,384]{2,1,0:T(1,128)} %bitcast), calls=%async_computation | async-start | bytes 393216 | tf_op jit(solution)/shard_map/all_to_all | solution.py:634
  27.4 31.9 %copy-start = (f32[1024,128]{1,0:T(8,128)S(1)}, f32[1024,128]{1,0:T(8,128)}, u32[]{:S(2)}) copy-start(f32[1024,128]{1,0:T(8,128)} %constant.19.clone.pair_ref) | copy-start | bytes 1572868
  43.4 44.2 %copy-start.5 = (bf16[512,2048]{1,0:T(8,128)(2,1)S(1)}, bf16[512,2048]{1,0:T(8,128)(2,1)}, u32[]{:S(2)}) copy-start(bf16[512,2048]{1,0:T(8,128)(2,1)} %get-tuple-element.34.second_ref) | copy-start | bytes 6291460
  45.6 42.0 %copy-start.1 = (f32[3,1,16,1024]{3,2,1,0:T(8,128)S(1)}, f32[3,1,16,1024]{3,2,1,0:T(8,128)}, u32[]{:S(2)}) copy-start(f32[3,1,16,1024]{3,2,1,0:T(8,128)} %cot_ref.1) | copy-start | bytes 589828
  45.7 41.9 %copy-start.2 = (s32[1,16,1024]{2,1,0:T(8,128)S(1)}, s32[1,16,1024]{2,1,0:T(8,128)}, u32[]{:S(2)}) copy-start(s32[1,16,1024]{2,1,0:T(8,128)} %mask_ref.1) | copy-start | bytes 196612
  45.7 41.9 %copy-start.3 = (f32[1536,128]{1,0:T(8,128)S(1)}, f32[1536,128]{1,0:T(8,128)}, u32[]{:S(2)}) copy-start(f32[1536,128]{1,0:T(8,128)} %constant.18.clone.turn_ref) | copy-start | bytes 2359300
  45.7 41.9 %copy-start.4 = (bf16[608,2048]{1,0:T(8,128)(2,1)S(1)}, bf16[608,2048]{1,0:T(8,128)(2,1)}, u32[]{:S(2)}) copy-start(bf16[608,2048]{1,0:T(8,128)(2,1)} %get-tuple-element.35.first_ref) | copy-start | bytes 7471108
